TPU v7x, 32 devices: a whole 2x2x4 slice. The times are simulated.
32 devices in a mesh: sec: 2 (over core), clu: 4 (over y, x), blk: 4 (over z).
Axes of the slice: x: 2, y: 2, z: 4, core: 2. Of those that a mesh axis runs over, the one named last changes fastest.
Arguments:
- right_side: float32 [32, 64, 32, 128], P(None, ('sec', 'clu'), 'blk'), may hold values from -18 to 18
- block_weight: float32 [64, 32], P(('sec', 'clu'), 'blk'), may hold values from 2 to 8
- across_weight: float32 [64, 32], P(('sec', 'clu'), 'blk'), may hold values from 0.3 to 1
- along_weight: float32 [64, 32], P(('sec', 'clu'), 'blk'), may hold values from 0.3 to 1
- block_stiffness: bfloat16 [128, 128], replicated, may hold values from -0.1 to 1.1, as said below
- across_matrix: bfloat16 [128, 128], replicated, may hold values from -0.044194174 to 0.044194174
- along_matrix: bfloat16 [128, 128], replicated, may hold values from -0.044194174 to 0.044194174
- boundary_blocks: bfloat16 [2, 4, 192, 128, 128], P('sec', 'clu', 'blk'), may hold values from -0.22949219 to 0.22949219
- block_rows: int32 [2, 4, 192], P('sec', 'clu', 'blk'), may hold values from 0 to 7
- block_columns: int32 [2, 4, 192], P('sec', 'clu', 'blk'), may hold values from 0 to 7
- live_pairs: int32 [2, 4, 4], P('sec', 'clu', 'blk'), may hold values from 12 to 48, as said below
- surface_index: int32 [2, 4, 512], P('sec', 'clu', 'blk'), may hold values from 0 to 8191, as said below
- interface_slot: int32 [4096], P('clu'), may hold values from 0 to 1023, as said below
Outputs:
- solution: float32 [32, 64, 32, 128], P(None, ('sec', 'clu'), 'blk')
Inputs may be any that keep to these rules, and one draw needn't show every extreme that they name: `block_stiffness`: symmetric. The first live_pairs[s, c, j] of a device's 48 listed pairs are live; some device has all 48 live. `surface_index`: the 128 entries of one device are distinct local dof numbers of that device. `interface_slot`: within each row range of 1024 interface dofs, each slot is taken exactly once.
All inputs are finite; a program needn't handle non-finite values.
Results may differ from a plain program's by a relative error of at most 0.0003.
The roundings to bfloat16 on the way count: a program that leaves them out, or rounds other values in their place, can miss the bound.
Values may be sent and summed in bfloat16 or wider, within the bound.
A program may use at most 64 MiB of HBM per device.

v0:
```python
import jax
import jax.numpy as jnp
from jax import lax
from jax.sharding import PartitionSpec as P

ITERS = 3


def passed_along(value, axis, by):
    count = lax.axis_size(axis)
    pairs = [(i, i + by) for i in range(count) if 0 <= i + by < count]
    return lax.ppermute(value, axis, pairs)


def extended_2(block, sides, width):
    for axis, dim in sides:
        count = lax.axis_size(axis)
        forward = [(i, i + 1) for i in range(count - 1)]
        backward = [(target, source) for source, target in forward]
        low = lax.ppermute(
            lax.slice_in_dim(block, block.shape[dim] - width, None, axis=dim), axis, forward
        )
        high = lax.ppermute(lax.slice_in_dim(block, 0, width, axis=dim), axis, backward)
        block = jnp.concatenate([low, block, high], axis=dim)
    return block


def case_sum(left, right):
    return jnp.sum(left * right, axis=(1, 2, 3))


def squares(residual):
    return lax.psum(case_sum(residual, residual), ("sec", "clu", "blk"))


def shards(
    right_side,
    block_weight,
    across_weight,
    along_weight,
    block_stiffness,
    across_matrix,
    along_matrix,
    boundary_blocks,
    block_rows,
    block_columns,
    live_pairs,
    surface_index,
    interface_slot,
):
    count_cases = right_side.shape[0]
    block_width = right_side.shape[3]
    across_edge = passed_along(across_weight[-1:, :], ("sec", "clu"), 1)
    across_lower = jnp.concatenate([across_edge, across_weight[:-1, :]], axis=0)
    along_edge = passed_along(along_weight[:, -1:], "blk", 1)
    along_lower = jnp.concatenate([along_edge, along_weight[:, :-1]], axis=1)
    coupled = jnp.concatenate(
        [across_matrix, across_matrix.T, along_matrix, along_matrix.T], axis=1
    )
    rows_local = block_rows[0, 0]
    columns_local = block_columns[0, 0]
    blocks_local = boundary_blocks[0, 0]
    surface_local = surface_index[0, 0]
    pair_count = rows_local.shape[0]
    cluster = blocks_local.shape[-1]
    surface_count = surface_local.shape[0]
    slot_count = interface_slot.shape[0]
    row_clusters = slot_count // cluster
    column_clusters = surface_count * lax.axis_size("sec") * lax.axis_size("clu") // cluster
    live_mask = (jnp.arange(pair_count, dtype=jnp.int32) < live_pairs[0, 0, 0]).astype(jnp.float32)
    row_onehot = (rows_local[:, None] == jnp.arange(row_clusters, dtype=jnp.int32)[None, :]).astype(
        jnp.float32
    ) * live_mask[:, None]
    column_onehot = (
        columns_local[:, None] == jnp.arange(column_clusters, dtype=jnp.int32)[None, :]
    ).astype(jnp.float32) * live_mask[:, None]
    inverse = (
        jnp.zeros((slot_count,), jnp.int32)
        .at[interface_slot]
        .set(jnp.arange(slot_count, dtype=jnp.int32))
    )
    solution = jnp.zeros_like(right_side)
    residual = right_side
    direction = right_side
    norm_now = squares(residual)
    for iteration in range(ITERS):
        rounded = direction.astype(jnp.bfloat16)
        extended = extended_2(rounded, ((("sec", "clu"), 1), ("blk", 2)), 1)
        own_part = jnp.einsum(
            "cabk,kl->cabl", rounded, block_stiffness, preferred_element_type=jnp.float32
        )
        neighbour = jnp.einsum(
            "cabk,kl->cabl", extended, coupled, preferred_element_type=jnp.float32
        )
        result = block_weight[None, :, :, None] * own_part
        result = result - across_weight[None, :, :, None] * neighbour[:, 2:, 1:-1, 0:block_width]
        result = (
            result
            - across_lower[None, :, :, None]
            * neighbour[:, :-2, 1:-1, block_width : 2 * block_width]
        )
        result = (
            result
            - along_weight[None, :, :, None]
            * neighbour[:, 1:-1, 2:, 2 * block_width : 3 * block_width]
        )
        result = result - along_lower[None, :, :, None] * neighbour[:, 1:-1, :-2, 3 * block_width :]
        mine = jnp.take(rounded.reshape(count_cases, -1), surface_local, axis=1)
        gathered = lax.all_gather(mine, ("sec", "blk"), axis=1, tiled=True)
        interface = jnp.take(gathered, interface_slot, axis=1).reshape(
            count_cases, row_clusters, cluster
        )
        picked = jnp.take(interface, rows_local, axis=1)
        terms = jnp.einsum("cpk,pkl->cpl", picked, blocks_local, preferred_element_type=jnp.float32)
        partial_columns = jnp.einsum(
            "cpl,pq->cql", terms, column_onehot, precision=lax.Precision.HIGHEST
        )
        columns = lax.psum(partial_columns, ("sec", "clu")).astype(jnp.bfloat16)
        chosen = jnp.take(columns, columns_local, axis=1)
        returned = jnp.einsum(
            "cpl,pkl->cpk", chosen, blocks_local, preferred_element_type=jnp.float32
        )
        partial_rows = jnp.einsum(
            "cpk,pr->crk", returned, row_onehot, precision=lax.Precision.HIGHEST
        )
        partial_rows = partial_rows.reshape(count_cases, slot_count)
        own_values = lax.psum_scatter(
            jnp.take(partial_rows, inverse, axis=1), ("sec", "blk"), scatter_dimension=1, tiled=True
        )
        image_field = (
            result.reshape(count_cases, -1)
            .at[:, surface_local]
            .add(own_values)
            .reshape(result.shape)
        )
        curvature = lax.psum(case_sum(direction, image_field), ("sec", "clu", "blk"))
        alpha = (norm_now / curvature)[:, None, None, None]
        solution = solution + alpha * direction
        if iteration + 1 < ITERS:
            residual = residual - alpha * image_field
            norm_next = squares(residual)
            direction = residual + (norm_next / norm_now)[:, None, None, None] * direction
            norm_now = norm_next
    return solution


def solution(mesh):
    return jax.shard_map(
        shards,
        mesh=mesh,
        in_specs=(
            P(None, ("sec", "clu"), "blk", None),
            P(("sec", "clu"), "blk"),
            P(("sec", "clu"), "blk"),
            P(("sec", "clu"), "blk"),
            P(),
            P(),
            P(),
            P("sec", "clu", "blk", None, None),
            P("sec", "clu", "blk"),
            P("sec", "clu", "blk"),
            P("sec", "clu", "blk"),
            P("sec", "clu", "blk"),
            P("clu"),
        ),
        out_specs=P(None, ("sec", "clu"), "blk", None),
        check_vma=False,
    )
```

profile of v0, /device:TPU:0, one launch (start us, length us, event | category | flops | bytes accessed | tf_op | source)
XLA Modules:
  0.0 644.7 jit_solution(6813380754361967349)
XLA Ops:
  6.5 2.0 copy.211
  9.9 5.5 collective-permute-start
  16.0 4.6 collective-permute-start.5
  21.2 4.8 collective-permute-start.4
  27.9 4.3 scatter_custom_fusion
  32.3 2.5 gather_fusion
  34.9 25.3 %all_gather.9 = bf16[32,1024]{0,1:T(8,128)(2,1)S(1)} all-gather(bf16[32,128]{0,1:T(8,128)(2,1)S(1)} %select_bitcast_fusion.5), channel_id=1, replica_groups=mesh['sec'=2,'clu'=4,'blk'=4] {'sec','blk'}, dimensions={1}, use_global_device_ids=true | all-gather | bytes 73728 | tf_op jit(solution)/shard_map/all_gather | solution.py:109
  60.8 3.2 gather_fusion.1
  64.3 2.0 gather_fusion.2
  66.3 2.1 fusion.24
  69.3 28.1 %all-reduce.4 = bf16[32,8,128]{2,0,1:T(8,128)(2,1)S(1)} all-reduce(f32[32,8,128]{2,0,1:T(8,128)S(1)} %bitcast.189), channel_id=1, replica_groups=mesh['sec'=2,'clu'=4,'blk'=4] {'sec','clu'}, use_global_device_ids=true, to_apply=%region_2.6 | all-reduce | flops 32768 | bytes 196608 | tf_op jit(solution)/shard_map/psum | solution.py:118
  100.2 2.8 gather_fusion.4
  107.0 4.7 collective-permute-start.2
  112.5 2.3 collective-permute-done.2
  116.6 2.8 fusion.45
  119.4 2.7 copy.95
  122.1 13.0 %reduce-scatter.4.cloned.1.call-done = f32[32,128]{0,1:T(8,128)} async-done(((f32[32,1024]{0,1:T(8,128)}), f32[32,128]{0,1:T(8,128)}) %reduce-scatter.4.cloned.1.call-update) | async-done | bytes 16400 | tf_op jit(solution)/shard_map/reduce_scatter | solution.py:127
  135.1 5.6 scatter_custom_fusion.1
  140.7 3.6 copy.57
  144.3 3.8 copy.98
  149.7 38.2 %all-reduce = (f32[32]{0:T(128)S(1)}, f32[32]{0:T(128)S(1)}) all-reduce(f32[32]{0:T(128)S(1)} %get-tuple-element.8, f32[32]{0:T(128)S(1)} %get-tuple-element.6), channel_id=1, replica_groups=mesh['sec'=2,'clu'=4,'blk'=4] {'sec','clu','blk'}, use_global_device_ids=true, to_apply=%region_1.0 | all-reduce | flops 64 | bytes 512 | tf_op jit(solution)/shard_map/psum | solution.py:33
  187.8 3.0 multiply_reduce_fusion.3
  190.8 40.7 %psum.66 = f32[32]{0:T(128)S(1)} all-reduce(f32[32]{0:T(128)S(1)} %get-tuple-element.17), channel_id=1, replica_groups=mesh['sec'=2,'clu'=4,'blk'=4] {'sec','clu','blk'}, use_global_device_ids=true, to_apply=%region_9.14 | all-reduce | flops 32 | bytes 256 | tf_op jit(solution)/shard_map/psum | solution.py:33
  232.0 2.9 fusion.167
  238.6 5.4 collective-permute-start.6
  244.1 2.6 gather_fusion.5
  246.8 25.7 %all_gather.10 = bf16[32,1024]{0,1:T(8,128)(2,1)S(1)} all-gather(bf16[32,128]{0,1:T(8,128)(2,1)S(1)} %select_bitcast_fusion.4), channel_id=1, replica_groups=mesh['sec'=2,'clu'=4,'blk'=4] {'sec','blk'}, dimensions={1}, use_global_device_ids=true | all-gather | bytes 73728 | tf_op jit(solution)/shard_map/all_gather | solution.py:109
  272.4 4.3 gather_fusion.6
  277.9 2.1 gather_fusion.7
  280.0 2.1 fusion.29
  283.0 28.8 %all-reduce.5 = bf16[32,8,128]{2,0,1:T(8,128)(2,1)S(1)} all-reduce(f32[32,8,128]{2,0,1:T(8,128)S(1)} %bitcast.190), channel_id=1, replica_groups=mesh['sec'=2,'clu'=4,'blk'=4] {'sec','clu'}, use_global_device_ids=true, to_apply=%region_10.15 | all-reduce | flops 32768 | bytes 196608 | tf_op jit(solution)/shard_map/psum | solution.py:118
  313.3 2.0 fusion.7
  317.3 5.0 gather_fusion.9
  325.0 4.5 collective-permute-start.8
  329.5 2.1 select_bitcast_fusion.1
  331.7 1.9 fusion.58
  334.3 3.8 fusion.42
  338.1 3.6 copy.100
  341.8 19.8 %reduce-scatter.6.cloned.1.call-done = f32[32,128]{0,1:T(8,128)} async-done(((f32[32,1024]{0,1:T(8,128)}), f32[32,128]{0,1:T(8,128)}) %reduce-scatter.6.cloned.1.call-update) | async-done | bytes 16400 | tf_op jit(solution)/shard_map/reduce_scatter | solution.py:127
  361.6 5.6 scatter_custom_fusion.2
  367.2 3.6 copy.70
  372.6 39.1 %psum.68 = f32[32]{0:T(128)S(1)} all-reduce(f32[32]{0:T(128)S(1)} %multiply_reduce_fusion.2), channel_id=1, replica_groups=mesh['sec'=2,'clu'=4,'blk'=4] {'sec','clu','blk'}, use_global_device_ids=true, to_apply=%region_14.19 | all-reduce | flops 32 | bytes 256 | tf_op jit(solution)/shard_map/psum | solution.py:136
  411.7 1.9 multiply_reduce_fusion.1
  413.6 40.6 %psum.69 = f32[32]{0:T(128)S(1)} all-reduce(f32[32]{0:T(128)S(1)} %multiply_reduce_fusion.1), channel_id=1, replica_groups=mesh['sec'=2,'clu'=4,'blk'=4] {'sec','clu','blk'}, use_global_device_ids=true, to_apply=%region_16.21 | all-reduce | flops 32 | bytes 256 | tf_op jit(solution)/shard_map/psum | solution.py:33
  454.2 3.3 fusion.166
  461.1 5.4 collective-permute-start.10
  466.6 2.6 gather_fusion.10
  469.3 25.4 %all_gather.11 = bf16[32,1024]{0,1:T(8,128)(2,1)S(1)} all-gather(bf16[32,128]{0,1:T(8,128)(2,1)S(1)} %select_bitcast_fusion.3), channel_id=1, replica_groups=mesh['sec'=2,'clu'=4,'blk'=4] {'sec','blk'}, dimensions={1}, use_global_device_ids=true | all-gather | bytes 73728 | tf_op jit(solution)/shard_map/all_gather | solution.py:109
  494.7 4.3 gather_fusion.11
  500.1 2.1 gather_fusion.12
  502.2 2.1 fusion.34
  505.3 28.8 %all-reduce.6 = bf16[32,8,128]{2,0,1:T(8,128)(2,1)S(1)} all-reduce(f32[32,8,128]{2,0,1:T(8,128)S(1)} %bitcast.191), channel_id=1, replica_groups=mesh['sec'=2,'clu'=4,'blk'=4] {'sec','clu'}, use_global_device_ids=true, to_apply=%region_17.22 | all-reduce | flops 32768 | bytes 196608 | tf_op jit(solution)/shard_map/psum | solution.py:118
  535.6 2.0 fusion.4
  539.5 5.0 gather_fusion.14
  547.2 4.5 collective-permute-start.12
  551.8 2.1 select_bitcast_fusion
  553.9 1.9 fusion.68
  556.5 3.8 fusion.39
  560.3 3.6 copy.106
  563.9 19.9 %reduce-scatter.8.cloned.1.call-done = f32[32,128]{0,1:T(8,128)} async-done(((f32[32,1024]{0,1:T(8,128)}), f32[32,128]{0,1:T(8,128)}) %reduce-scatter.8.cloned.1.call-update) | async-done | bytes 16400 | tf_op jit(solution)/shard_map/reduce_scatter | solution.py:127
  583.8 5.7 scatter_custom_fusion.3
  589.6 3.6 copy.82
  595.0 39.1 %psum.71 = f32[32]{0:T(128)S(1)} all-reduce(f32[32]{0:T(128)S(1)} %multiply_reduce_fusion), channel_id=1, replica_groups=mesh['sec'=2,'clu'=4,'blk'=4] {'sec','clu','blk'}, use_global_device_ids=true, to_apply=%region_21.26 | all-reduce | flops 32 | bytes 256 | tf_op jit(solution)/shard_map/psum | solution.py:136
  634.1 2.2 multiply_add_fusion
  (194 shorter events, 47.6 us)
Async XLA Ops:
  6.5 59.7 %copy-start = (bf16[1,1,48,128,128]{4,3,2,1,0:T(8,128)(2,1)S(1)}, bf16[1,1,48,128,128]{4,3,2,1,0:T(8,128)(2,1)}, u32[]{:S(2)}) copy-start(bf16[1,1,48,128,128]{4,3,2,1,0:T(8,128)(2,1)} %param.28) | copy-start | bytes 4718596
  6.5 8.8 %copy-start.7 = (f32[8,8]{1,0:T(8,128)S(1)}, f32[8,8]{1,0:T(8,128)}, u32[]{:S(2)}) copy-start(f32[8,8]{1,0:T(8,128)} %param.24) | copy-start | bytes 772
  6.5 14.1 %copy-start.8 = (f32[8,8]{1,0:T(8,128)S(1)}, f32[8,8]{1,0:T(8,128)}, u32[]{:S(2)}) copy-start(f32[8,8]{1,0:T(8,128)} %param.23) | copy-start | bytes 772
  6.5 128.5 %reduce-scatter.4.cloned.1.call-start = ((), (), s32[]{:S(2)}) async-start(), calls=%async_computation.3 | async-start | bytes 589824 | tf_op jit(solution)/shard_map/reduce_scatter | solution.py:127
  8.5 19.2 %copy-start.46 = (s32[1,1,128]{2,1,0:T(1,128)S(1)}, s32[1,1,128]{2,1,0:T(1,128)}, u32[]{:S(2)}) copy-start(s32[1,1,128]{2,1,0:T(1,128)} %param.32) | copy-start | bytes 1540
  8.5 19.2 %copy-start.25 = (s32[1024]{0:T(1024)S(1)}, s32[1024]{0:T(1024)}, u32[]{:S(2)}) copy-start(s32[1024]{0:T(1024)} %param.33) | copy-start | bytes 12292
  8.5 19.3 %copy-start.32 = (s32[1,1,48]{2,1,0:T(1,128)S(1)}, s32[1,1,48]{2,1,0:T(1,128)}, u32[]{:S(2)}) copy-start(s32[1,1,48]{2,1,0:T(1,128)} %param.29) | copy-start | bytes 580
  8.5 19.3 %copy-start.29 = (s32[1,1,48]{2,1,0:T(1,128)S(1)}, s32[1,1,48]{2,1,0:T(1,128)}, u32[]{:S(2)}) copy-start(s32[1,1,48]{2,1,0:T(1,128)} %param.30) | copy-start | bytes 580
  8.6 97.1 %collective-permute-start.1 = (bf16[32,1,8,128]{3,0,2,1:T(8,128)(2,1)S(1)}, bf16[32,1,8,128]{3,0,2,1:T(8,128)(2,1)S(1)}, u32[]{:S(2)}, u32[]{:S(2)}) collective-permute-start(bf16[32,1,8,128]{3,0,2,1:T(8,128)(2,1)S(1)} %get-tuple-element.42), channel_id=1, source_target_pairs={{4,0},{8,4},{12,8},{16,12},{20,16},{24,20},{28,24},{5,1},{9,5},{13... | collective-permute-start | bytes 196616 | tf_op jit(solution)/shard_map/ppermute | solution.py:23
  9.9 95.8 %collective-permute-start = (bf16[32,1,8,128]{3,0,2,1:T(8,128)(2,1)S(1)}, bf16[32,1,8,128]{3,0,2,1:T(8,128)(2,1)S(1)}, u32[]{:S(2)}, u32[]{:S(2)}) collective-permute-start(bf16[32,1,8,128]{3,0,2,1:T(8,128)(2,1)S(1)} %get-tuple-element.41), channel_id=1, source_target_pairs={{0,4},{4,8},{8,12},{12,16},{16,20},{20,24},{24,28},{1,5},{5,9},{9,... | collective-permute-start | bytes 196616 | tf_op jit(solution)/shard_map/ppermute | solution.py:20
  16.0 88.9 %collective-permute-start.5 = (f32[8,1]{1,0:T(8,128)}, f32[8,1]{1,0:T(8,128)}, u32[]{:S(2)}, u32[]{:S(2)}) collective-permute-start(f32[8,1]{1,0:T(8,128)} %slice.93), channel_id=1, source_target_pairs={{0,1},{1,2},{2,3},{4,5},{5,6},{6,7},{8,9},{9,10},{10,11},{12,13},{... | collective-permute-start | bytes 104 | tf_op jit(solution)/shard_map/ppermute | solution.py:12
  21.2 90.5 %collective-permute-start.4 = (f32[1,8]{1,0:T(1,128)}, f32[1,8]{1,0:T(1,128)}, u32[]{:S(2)}, u32[]{:S(2)}) collective-permute-start(f32[1,8]{1,0:T(1,128)} %slice.89), channel_id=1, source_target_pairs={{0,4},{4,8},{8,12},{12,16},{16,20},{20,24},{24,28},{1,5},{5,9},{9,... | collective-permute-start | bytes 104 | tf_op jit(solution)/shard_map/ppermute | solution.py:12
  27.7 7.2 %copy-start.39 = (pred[128]{0:T(512)(128)(4,1)}, pred[128]{0:T(512)(128)(4,1)S(1)}, u32[]{:S(2)}) copy-start(pred[128]{0:T(512)(128)(4,1)S(1)} %compare_and_fusion.4) | copy-start | bytes 388
  27.8 40.5 %copy-start.24 = (pred[1024]{0:T(1024)(128)(4,1)}, pred[1024]{0:T(1024)(128)(4,1)S(1)}, u32[]{:S(2)}) copy-start(pred[1024]{0:T(1024)(128)(4,1)S(1)} %compare_and_fusion.1) | copy-start | bytes 3076
  27.8 40.5 %copy-start.38 = (pred[48]{0:T(512)(128)(4,1)}, pred[48]{0:T(512)(128)(4,1)S(1)}, u32[]{:S(2)}) copy-start(pred[48]{0:T(512)(128)(4,1)S(1)} %compare_and_fusion.3) | copy-start | bytes 148
  27.9 70.2 %copy-start.35 = (pred[48]{0:T(512)(128)(4,1)}, pred[48]{0:T(512)(128)(4,1)S(1)}, u32[]{:S(2)}) copy-start(pred[48]{0:T(512)(128)(4,1)S(1)} %compare_and_fusion.2) | copy-start | bytes 148
  32.2 67.9 %copy-start.9 = (s32[1024]{0:T(1024)}, s32[1024]{0:T(1024)S(1)}, u32[]{:S(2)}) copy-start(s32[1024]{0:T(1024)S(1)} %fusion.129) | copy-start | bytes 12292
  32.2 70.7 %copy-start.21 = (pred[1024]{0:T(1024)(128)(4,1)}, pred[1024]{0:T(1024)(128)(4,1)S(1)}, u32[]{:S(2)}) copy-start(pred[1024]{0:T(1024)(128)(4,1)S(1)} %compare_and_fusion) | copy-start | bytes 3076
  32.3 36.0 %copy-start.26 = (s32[1024]{0:T(1024)}, s32[1024]{0:T(1024)S(1)}, u32[]{:S(2)}) copy-start(s32[1024]{0:T(1024)S(1)} %pad_clamp_fusion.2) | copy-start | bytes 12292
  60.2 8.2 %copy-start.27 = (s32[1024]{0:T(1024)}, s32[1024]{0:T(1024)S(1)}, u32[]{:S(2)}) copy-start(s32[1024]{0:T(1024)S(1)} %pad_clamp_fusion.1) | copy-start | bytes 12292
  60.8 38.2 %copy-start.18 = (f32[48]{0:T(128)}, f32[48]{0:T(128)S(1)}, u32[]{:S(2)}) copy-start(f32[48]{0:T(128)S(1)} %compare_convert_fusion) | copy-start | bytes 580
  97.4 1.6 copy-start.28
  99.9 4.7 copy-start.2
  100.1 4.6 copy-start.3
  104.0 257.6 %reduce-scatter.6.cloned.1.call-start = ((), (), s32[]{:S(2)}) async-start(), calls=%async_computation.4 | async-start | bytes 589824 | tf_op jit(solution)/shard_map/reduce_scatter | solution.py:127
  105.7 6.9 %collective-permute-start.3 = (bf16[32,10,1,128]{3,0,2,1:T(8,128)(2,1)S(1)}, bf16[32,10,1,128]{3,0,2,1:T(8,128)(2,1)S(1)}, u32[]{:S(2)}, u32[]{:S(2)}) collective-permute-start(bf16[32,10,1,128]{3,0,2,1:T(8,128)(2,1)S(1)} %get-tuple-element.36), channel_id=1, source_target_pairs={{1,0},{2,1},{3,2},{5,4},{6,5},{7,6},{9,8},{10,9},{11,10},{13,12},{... | collective-permute-start | bytes 245768 | tf_op jit(solution)/shard_map/ppermute | solution.py:23
  107.0 7.9 %collective-permute-start.2 = (bf16[32,10,1,128]{3,0,2,1:T(8,128)(2,1)S(1)}, bf16[32,10,1,128]{3,0,2,1:T(8,128)(2,1)S(1)}, u32[]{:S(2)}, u32[]{:S(2)}) collective-permute-start(bf16[32,10,1,128]{3,0,2,1:T(8,128)(2,1)S(1)} %get-tuple-element.35), channel_id=1, source_target_pairs={{0,1},{1,2},{2,3},{4,5},{5,6},{6,7},{8,9},{9,10},{10,11},{12,13},{... | collective-permute-start | bytes 245768 | tf_op jit(solution)/shard_map/ppermute | solution.py:20
  112.3 4.1 copy-start.12
  115.8 0.8 copy-start.4
  115.9 0.8 copy-start.15
  144.3 3.8 copy-start.1
  187.8 3.0 copy-start.44
  234.9 11.8 %copy-start.40 = (pred[128]{0:T(512)(128)(4,1)S(1)}, pred[128]{0:T(512)(128)(4,1)}, u32[]{:S(2)}) copy-start(pred[128]{0:T(512)(128)(4,1)} %copy-done.39) | copy-start | bytes 388
  237.3 85.0 %collective-permute-start.7 = (bf16[32,1,8,128]{3,0,2,1:T(8,128)(2,1)}, bf16[32,1,8,128]{3,0,2,1:T(8,128)(2,1)}, u32[]{:S(2)}, u32[]{:S(2)}) collective-permute-start(bf16[32,1,8,128]{3,0,2,1:T(8,128)(2,1)} %get-tuple-element.40), channel_id=1, source_target_pairs={{4,0},{8,4},{12,8},{16,12},{20,16},{24,20},{28,24},{5,1},{9,5},{13... | collective-permute-start | bytes 196616 | tf_op jit(solution)/shard_map/ppermute | solution.py:23
  238.6 83.7 %collective-permute-start.6 = (bf16[32,1,8,128]{3,0,2,1:T(8,128)(2,1)}, bf16[32,1,8,128]{3,0,2,1:T(8,128)(2,1)}, u32[]{:S(2)}, u32[]{:S(2)}) collective-permute-start(bf16[32,1,8,128]{3,0,2,1:T(8,128)(2,1)} %get-tuple-element.39), channel_id=1, source_target_pairs={{0,4},{4,8},{8,12},{12,16},{16,20},{20,24},{24,28},{1,5},{5,9},{9,... | collective-permute-start | bytes 196616 | tf_op jit(solution)/shard_map/ppermute | solution.py:20
  280.0 2.1 copy-start.19
  280.0 2.1 copy-start.30
  282.1 31.3 %copy-start.36 = (pred[48]{0:T(512)(128)(4,1)S(1)}, pred[48]{0:T(512)(128)(4,1)}, u32[]{:S(2)}) copy-start(pred[48]{0:T(512)(128)(4,1)} %copy-done.35) | copy-start | bytes 148
  313.3 2.0 copy-start.33
  313.3 3.9 copy-start.10
  315.3 14.2 %copy-start.22 = (pred[1024]{0:T(1024)(128)(4,1)S(1)}, pred[1024]{0:T(1024)(128)(4,1)}, u32[]{:S(2)}) copy-start(pred[1024]{0:T(1024)(128)(4,1)} %copy-done.21) | copy-start | bytes 3076
  323.7 8.0 %collective-permute-start.9 = (bf16[32,10,1,128]{3,0,2,1:T(8,128)(2,1)}, bf16[32,10,1,128]{3,0,2,1:T(8,128)(2,1)S(1)}, u32[]{:S(2)}, u32[]{:S(2)}) collective-permute-start(bf16[32,10,1,128]{3,0,2,1:T(8,128)(2,1)} %get-tuple-element.34), channel_id=1, source_target_pairs={{1,0},{2,1},{3,2},{5,4},{6,5},{7,6},{9,8},{10,9},{11,10},{13,12},{... | collective-permute-start | bytes 245768 | tf_op jit(solution)/shard_map/ppermute | solution.py:23
  325.0 6.7 %collective-permute-start.8 = (bf16[32,10,1,128]{3,0,2,1:T(8,128)(2,1)S(1)}, bf16[32,10,1,128]{3,0,2,1:T(8,128)(2,1)S(1)}, u32[]{:S(2)}, u32[]{:S(2)}) collective-permute-start(bf16[32,10,1,128]{3,0,2,1:T(8,128)(2,1)S(1)} %get-tuple-element.33), channel_id=1, source_target_pairs={{0,1},{1,2},{2,3},{4,5},{5,6},{6,7},{8,9},{9,10},{10,11},{12,13},{... | collective-permute-start | bytes 245768 | tf_op jit(solution)/shard_map/ppermute | solution.py:20
  331.6 252.2 %reduce-scatter.8.cloned.1.call-start = ((), (), s32[]{:S(2)}) async-start(), calls=%async_computation.5 | async-start | bytes 589824 | tf_op jit(solution)/shard_map/reduce_scatter | solution.py:127
  333.6 0.8 copy-start.5
  333.6 0.8 copy-start.13
  370.8 40.9 %copy-start.50 = (f32[32]{0:T(128)S(1)}, f32[32]{0:T(128)}, u32[]{:S(2)}) copy-start(f32[32]{0:T(128)} %copy-done.49) | copy-start | bytes 388
  411.7 45.8 %copy-start.42 = (f32[32]{0:T(128)}, f32[32]{0:T(128)S(1)}, u32[]{:S(2)}) copy-start(f32[32]{0:T(128)S(1)} %div.17) | copy-start | bytes 388
  454.2 3.3 copy-start.47
  457.4 11.8 %copy-start.41 = (pred[128]{0:T(512)(128)(4,1)S(1)}, pred[128]{0:T(512)(128)(4,1)}, u32[]{:S(2)}) copy-start(pred[128]{0:T(512)(128)(4,1)} %copy-done.39) | copy-start | bytes 388
  459.8 84.7 %collective-permute-start.11 = (bf16[32,1,8,128]{3,0,2,1:T(8,128)(2,1)}, bf16[32,1,8,128]{3,0,2,1:T(8,128)(2,1)}, u32[]{:S(2)}, u32[]{:S(2)}) collective-permute-start(bf16[32,1,8,128]{3,0,2,1:T(8,128)(2,1)} %get-tuple-element.38), channel_id=1, source_target_pairs={{4,0},{8,4},{12,8},{16,12},{20,16},{24,20},{28,24},{5,1},{9,5},{13... | collective-permute-start | bytes 196616 | tf_op jit(solution)/shard_map/ppermute | solution.py:23
  461.1 83.4 %collective-permute-start.10 = (bf16[32,1,8,128]{3,0,2,1:T(8,128)(2,1)}, bf16[32,1,8,128]{3,0,2,1:T(8,128)(2,1)}, u32[]{:S(2)}, u32[]{:S(2)}) collective-permute-start(bf16[32,1,8,128]{3,0,2,1:T(8,128)(2,1)} %get-tuple-element.37), channel_id=1, source_target_pairs={{0,4},{4,8},{8,12},{12,16},{16,20},{20,24},{24,28},{1,5},{5,9},{9,... | collective-permute-start | bytes 196616 | tf_op jit(solution)/shard_map/ppermute | solution.py:20
  502.2 2.1 copy-start.20
  502.2 2.1 copy-start.31
  504.3 31.3 %copy-start.37 = (pred[48]{0:T(512)(128)(4,1)S(1)}, pred[48]{0:T(512)(128)(4,1)}, u32[]{:S(2)}) copy-start(pred[48]{0:T(512)(128)(4,1)} %copy-done.35) | copy-start | bytes 148
  535.6 2.0 copy-start.34
  535.6 3.9 copy-start.11
  537.5 14.2 %copy-start.23 = (pred[1024]{0:T(1024)(128)(4,1)S(1)}, pred[1024]{0:T(1024)(128)(4,1)}, u32[]{:S(2)}) copy-start(pred[1024]{0:T(1024)(128)(4,1)} %copy-done.21) | copy-start | bytes 3076
  545.9 7.9 %collective-permute-start.13 = (bf16[32,10,1,128]{3,0,2,1:T(8,128)(2,1)}, bf16[32,10,1,128]{3,0,2,1:T(8,128)(2,1)S(1)}, u32[]{:S(2)}, u32[]{:S(2)}) collective-permute-start(bf16[32,10,1,128]{3,0,2,1:T(8,128)(2,1)} %get-tuple-element.32), channel_id=1, source_target_pairs={{1,0},{2,1},{3,2},{5,4},{6,5},{7,6},{9,8},{10,9},{11,10},{13,12},{... | collective-permute-start | bytes 245768 | tf_op jit(solution)/shard_map/ppermute | solution.py:23
  547.2 6.7 %collective-permute-start.12 = (bf16[32,10,1,128]{3,0,2,1:T(8,128)(2,1)S(1)}, bf16[32,10,1,128]{3,0,2,1:T(8,128)(2,1)S(1)}, u32[]{:S(2)}, u32[]{:S(2)}) collective-permute-start(bf16[32,10,1,128]{3,0,2,1:T(8,128)(2,1)S(1)} %get-tuple-element.31), channel_id=1, source_target_pairs={{0,1},{1,2},{2,3},{4,5},{5,6},{6,7},{8,9},{9,10},{10,11},{12,13},{... | collective-permute-start | bytes 245768 | tf_op jit(solution)/shard_map/ppermute | solution.py:20
  555.7 0.8 copy-start.6
  593.2 40.9 %copy-start.48 = (f32[32]{0:T(128)S(1)}, f32[32]{0:T(128)}, u32[]{:S(2)}) copy-start(f32[32]{0:T(128)} %copy-done.47) | copy-start | bytes 388
  593.2 40.9 %copy-start.43 = (f32[32]{0:T(128)S(1)}, f32[32]{0:T(128)}, u32[]{:S(2)}) copy-start(f32[32]{0:T(128)} %copy-done.42) | copy-start | bytes 388
  593.2 40.9 %copy-start.45 = (f32[32]{0:T(128)S(1)}, f32[32]{0:T(128)}, u32[]{:S(2)}) copy-start(f32[32]{0:T(128)} %copy-done.44) | copy-start | bytes 388
  (4 other events, 2.8 us)
Sparse Core Ops, SparseCore 0:
  104.1 30.8 reduce-scatter.3
  331.7 29.8 reduce-scatter.5
  554.0 29.8 reduce-scatter.7
where the time goes:
time: 653 us; the launch traced here: 645 us
  blocking collectives  360 us (55%)
  local copies, waits for them, and re-layouts  87.8 us (13%)
  waiting for transfers between devices  55.3 us (8%)
  other arithmetic  48 us (7%)
  starting transfers between devices  47.3 us (7%)
  matrix products  31.6 us (5%)
  between operations  14.9 us (2%)
    psum x3, blocking collectives, squares(): return lax.psum(case_sum(residual, residual), ('sec', 'clu', 'blk'))  119 us
    psum x3, blocking collectives, shards(): columns = lax.psum(partial_columns, ('sec', 'clu')).astype(jnp.bfloat16)  85.7 us
    psum x2, blocking collectives, shards(): lax.psum(case_sum(direction, image_field), ('sec', 'clu', 'blk'))  78.2 us
    all_gather x3, blocking collectives, shards(): gathered = lax.all_gather(mine, ('sec', 'blk'), axis=1, tiled=True)  76.3 us
    reduce_scatter x3, waiting for transfers between devices, shards(): lax.psum_scatter(jnp.take(partial_rows, inverse, axis=1), ('sec', 'blk'),...  52.7 us
    ppermute x6, starting transfers between devices, extended_2(): lax.ppermute(lax.slice_in_dim(block, block.shape[dim] - width, None, axis...  30.2 us
    scatter-add x3, other arithmetic, shards(): image_field = result.reshape(count_cases, -1).at[:, surface_local].add(ow...  16.9 us
    reshape x4, local copies, waits for them, and re-layouts, shards(): image_field = result.reshape(count_cases, -1).at[:, surface_local].add(ow...  14.6 us
  transfers between devices with their start and end apart: 17, of which 5 were waited for; matrix products, arithmetic and copies ran while one was open for 16% of the time, Pallas kernels for 0%

commit v1 on v0

v1 whole, which is shorter than its diff:
```python
import functools

import jax
import jax.numpy as jnp
from jax import lax
from jax.experimental import pallas as pl
from jax.experimental.pallas import tpu as pltpu
from jax.sharding import PartitionSpec as P

ITERS = 3
F32 = jnp.float32
BF16 = jnp.bfloat16
MESH = pl.DeviceIdType.MESH

TRACE, ZSUM, ZALL, YSUM, DOTS, UP, DOWN, LEFT, RIGHT = range(9)


def lanes(tile, index):
    return jnp.take_along_axis(tile, index, axis=1, mode="promise_in_bounds")


def kernel(
    axes,
    dims,
    rhs,
    weight,
    across,
    along,
    stiff,
    amat,
    lmat,
    blocks,
    rows,
    cols,
    live,
    surf,
    surf_inv,
    slot,
    slot_inv,
    out,
    direction,
    residual,
    image,
    total,
    rounded,
    side,
    across_ext,
    along_ext,
    traces,
    tiles,
    zpart,
    zrecv,
    zlow,
    ytile,
    ypart,
    yrecv,
    dot_send,
    dot_recv,
    send_sem,
    recv_sem,
    edge_send,
    edge_recv,
):
    n_sec, n_clu, n_blk = axes
    cases, bx, by, wide, pairs = dims
    n_slab, n_grp, n_all = n_sec * n_clu, n_sec * n_blk, n_sec * n_clu * n_blk
    sec, clu, blk = lax.axis_index("sec"), lax.axis_index("clu"), lax.axis_index("blk")
    slab = sec * n_clu + clu
    group = sec * n_blk + blk
    me = slab * n_blk + blk
    tile = (cases, wide)

    def slab_device(index):
        return (index // n_clu, lax.rem(index, n_clu), blk)

    def group_device(index):
        return (index // n_blk, clu, lax.rem(index, n_blk))

    def any_device(index):
        return (index // (n_clu * n_blk), lax.rem(index // n_blk, n_clu), lax.rem(index, n_blk))

    next_slab = slab_device(lax.rem(slab + 1, n_slab))
    last_slab = slab_device(lax.rem(slab + n_slab - 1, n_slab))
    next_blk = (sec, clu, lax.rem(blk + 1, n_blk))
    last_blk = (sec, clu, lax.rem(blk + n_blk - 1, n_blk))

    barrier = pltpu.get_barrier_semaphore()

    @pl.loop(1, n_all)
    def _(k):
        pl.semaphore_signal(
            barrier, inc=1, device_id=any_device(lax.rem(me + k, n_all)), device_id_type=MESH
        )

    def send(src, dst, it, phase, device):
        pltpu.make_async_remote_copy(
            src_ref=src,
            dst_ref=dst,
            send_sem=send_sem.at[it, phase],
            recv_sem=recv_sem.at[it, phase],
            device_id=device,
            device_id_type=MESH,
        ).start()

    def received(ref, it, phase):
        pltpu.make_async_copy(ref, ref, recv_sem.at[it, phase]).wait()

    def sent(ref, it, phase):
        pltpu.make_async_copy(ref, ref, send_sem.at[it, phase]).wait()

    surf_row = jnp.broadcast_to(surf[...], tile)
    surf_lane = lax.rem(surf_row, wide)
    surf_block = surf_row // wide
    zero = jnp.zeros(tile, F32)

    def begin(a, carry):
        square, trace = carry
        for b in range(by):
            i = a * by + b
            value = rhs[pl.ds(i, cases, stride=bx * by), :]
            direction[a, b] = value
            residual[a, b] = value
            total[a, b] = zero
            rounded[0, a + 1, b] = value.astype(BF16)
            square += value * value
            trace = jnp.where(surf_block == i, lanes(value, surf_lane), trace)
        return square, trace

    square, trace = lax.fori_loop(0, bx, begin, (zero, zero))
    traces[0, 0] = trace.astype(BF16)
    across_ext[1:bx] = across[: bx - 1]
    across_ext[bx] = across[bx - 1] * (slab < n_slab - 1).astype(F32)
    along_ext[1:by] = along[: by - 1]
    along_ext[by] = along[by - 1] * (blk < n_blk - 1).astype(F32)

    pl.semaphore_wait(barrier, n_all - 1)

    edges = (
        (across.at[bx - 1], across_ext.at[0], 0, next_slab),
        (along.at[by - 1], along_ext.at[0], 1, next_blk),
    )

    def edge_copy(src, dst, n, device):
        return pltpu.make_async_remote_copy(
            src_ref=src,
            dst_ref=dst,
            send_sem=edge_send.at[n],
            recv_sem=edge_recv.at[n],
            device_id=device,
            device_id_type=MESH,
        )

    def permuted(index_row, count, source):
        lane = lax.rem(index_row, wide)
        part = index_row // wide

        def step(k, value):
            found, number = source(k)
            return jnp.where(part == number, lanes(found, lane), value)

        return lax.fori_loop(0, count, step, zero, unroll=count if count <= 8 else 1)

    def pair_sums(pick, into, count, flip):
        unit = 8 if pairs % 8 == 0 else 1

        def step(i, sums):
            sums = list(sums)
            for u in range(unit):
                e = i * unit + u
                left = pick(e)
                dims_ = (((1,), (1 if flip else 0,)), ((), ()))
                term = lax.dot_general(left, blocks[e], dims_, preferred_element_type=F32)
                goal = jnp.where(e < live[0, 0], into[0, e], -1)
                sums = [s + jnp.where(goal == q, term, zero) for q, s in enumerate(sums)]
            return tuple(sums)

        return lax.fori_loop(0, pairs // unit, step, (zero,) * count)

    sublane = lax.broadcasted_iota(jnp.int32, tile, 0)
    lane_id = lax.broadcasted_iota(jnp.int32, tile, 1)

    def iteration(it, square, first, last):
        @pl.loop(1, n_grp)
        def _(k):
            target = lax.rem(group + k, n_grp)
            send(traces.at[it, 0], traces.at[it, k], it, TRACE, group_device(target))

        send(rounded.at[it, bx], rounded.at[it, 0], it, UP, next_slab)
        send(rounded.at[it, 1], rounded.at[it, bx + 1], it, DOWN, last_slab)
        send(rounded.at[it, pl.ds(1, bx), by - 1], side.at[it, 0], it, RIGHT, next_blk)
        send(rounded.at[it, pl.ds(1, bx), 0], side.at[it, 1], it, LEFT, last_blk)

        @pl.loop(0, bx)
        def _(a):
            own = rounded[it, a + 1].reshape(by * cases, wide)
            part = jnp.dot(own, stiff[...], preferred_element_type=F32)
            image[a] = weight[a] * part.reshape(by, cases, wide)

        received(traces.at[it, pl.ds(1, n_grp - 1)], it, TRACE)

        @pl.loop(0, n_grp)
        def _(r):
            def source(k):
                return traces[it, k].astype(F32), lax.rem(group - k + n_grp, n_grp)

            index = jnp.broadcast_to(slot[pl.ds(r, 1), :], tile)
            tiles[r] = permuted(index, n_grp, source).astype(BF16)

        sums = pair_sums(lambda e: tiles[rows[0, e]], cols, n_slab, False)
        for q in range(n_slab):
            zpart[it, q] = sums[q]

        @pl.loop(1, n_slab)
        def _(k):
            target = lax.rem(slab + k, n_slab)
            send(zpart.at[it, target], zrecv.at[it, k - 1], it, ZSUM, slab_device(target))

        received(rounded.at[it, 0], it, UP)
        received(rounded.at[it, bx + 1], it, DOWN)
        received(side.at[it, 0], it, RIGHT)
        received(side.at[it, 1], it, LEFT)

        @pl.loop(0, bx)
        def _(a):
            after = rounded[it, a + 2].reshape(by * cases, wide)
            before = rounded[it, a].reshape(by * cases, wide)
            part = jnp.dot(after, amat[...], preferred_element_type=F32)
            value = image[a] - across_ext[a + 1] * part.reshape(by, cases, wide)
            part = lax.dot_general(
                before, amat[...], (((1,), (1,)), ((), ())), preferred_element_type=F32
            )
            image[a] = value - across_ext[a] * part.reshape(by, cases, wide)

        received(zrecv.at[it], it, ZSUM)
        column = zpart[it, slab]
        for k in range(n_slab - 1):
            column += zrecv[it, k]
        zlow[it, 0] = column.astype(BF16)

        @pl.loop(1, n_slab)
        def _(k):
            target = lax.rem(slab + k, n_slab)
            send(zlow.at[it, 0], zlow.at[it, k], it, ZALL, slab_device(target))

        @pl.loop(0, bx)
        def _(a):
            right = rounded[it, a + 1, pl.ds(1, by - 1)].reshape((by - 1) * cases, wide)
            left = rounded[it, a + 1, pl.ds(0, by - 1)].reshape((by - 1) * cases, wide)
            after = jnp.concatenate([right, side[it, 1, a]], axis=0)
            before = jnp.concatenate([side[it, 0, a], left], axis=0)
            part = jnp.dot(after, lmat[...], preferred_element_type=F32)
            value = image[a] - along_ext[pl.ds(1, by), a] * part.reshape(by, cases, wide)
            part = lax.dot_general(
                before, lmat[...], (((1,), (1,)), ((), ())), preferred_element_type=F32
            )
            image[a] = value - along_ext[pl.ds(0, by), a] * part.reshape(by, cases, wide)

        received(zlow.at[it, pl.ds(1, n_slab - 1)], it, ZALL)
        sums = pair_sums(
            lambda e: zlow[it, lax.rem(slab - cols[0, e] + n_slab, n_slab)], rows, n_grp, True
        )
        for r in range(n_grp):
            ytile[r] = sums[r]

        @pl.loop(0, n_grp)
        def _(g):
            index = jnp.broadcast_to(slot_inv[pl.ds(g, 1), :], tile)
            ypart[it, g] = permuted(index, n_grp, lambda k: (ytile[k], k))

        @pl.loop(1, n_grp)
        def _(k):
            target = lax.rem(group + k, n_grp)
            send(ypart.at[it, target], yrecv.at[it, k - 1], it, YSUM, group_device(target))

        received(yrecv.at[it], it, YSUM)
        own_y = ypart[it, group]
        for k in range(n_grp - 1):
            own_y += yrecv[it, k]

        def finish(a, carry):
            d_q, r_q, q_q = carry
            for b in range(by):
                index = jnp.broadcast_to(surf_inv[pl.ds(a * by + b, 1), :], tile)
                extra = lanes(own_y, jnp.maximum(index, 0))
                value = image[a, b] + jnp.where(index >= 0, extra, zero)
                image[a, b] = value
                d_q += direction[a, b] * value
                r_q += residual[a, b] * value
                q_q += value * value
            return d_q, r_q, q_q

        d_q, r_q, q_q = lax.fori_loop(0, bx, finish, (zero, zero, zero))

        packed = zero
        for m, value in enumerate((square, d_q, r_q, q_q)):
            case = jnp.broadcast_to(jnp.sum(value, axis=1, keepdims=True), tile)
            packed = jnp.where(lane_id == sublane + m * cases, case, packed)
        dot_send[it] = jnp.sum(packed, axis=0, keepdims=True)

        @pl.loop(1, n_all)
        def _(k):
            target = any_device(lax.rem(me + k, n_all))
            send(dot_send.at[it], dot_recv.at[it, k - 1], it, DOTS, target)

        received(dot_recv.at[it], it, DOTS)
        summed = dot_send[it] + jnp.sum(dot_recv[it], axis=0)
        summed = jnp.broadcast_to(summed, tile)

        def case_value(m):
            mine = jnp.where(lane_id == sublane + m * cases, summed, zero)
            return jnp.broadcast_to(jnp.sum(mine, axis=1, keepdims=True), tile)

        norm, d_q = case_value(0), case_value(1)
        alpha = norm / d_q
        if last:

            @pl.loop(0, bx)
            def _(a):
                for b in range(by):
                    value = total[a, b] + alpha * direction[a, b]
                    out[pl.ds(a * by + b, cases, stride=bx * by), :] = value

            return zero

        r_q, q_q = case_value(2), case_value(3)
        norm_next = norm - 2.0 * alpha * r_q + alpha * alpha * q_q
        beta = norm_next / norm

        def update(a, carry):
            square, trace = carry
            for b in range(by):
                old = direction[a, b]
                total[a, b] += alpha * old
                rest = residual[a, b] - alpha * image[a, b]
                residual[a, b] = rest
                square += rest * rest
                value = rest + beta * old
                direction[a, b] = value
                rounded[it + 1, a + 1, b] = value.astype(BF16)
                trace = jnp.where(surf_block == a * by + b, lanes(value, surf_lane), trace)
            return square, trace

        square, trace = lax.fori_loop(0, bx, update, (zero, zero))
        traces[it + 1, 0] = trace.astype(BF16)
        return square

    for edge in edges:
        edge_copy(*edge).start()
    for edge in edges:
        edge_copy(*edge).wait()
    across_ext[0] = across_ext[0] * (slab > 0).astype(F32)
    along_ext[0] = along_ext[0] * (blk > 0).astype(F32)

    square = lax.fori_loop(0, ITERS - 1, lambda it, s: iteration(it, s, False, False), square)
    iteration(ITERS - 1, square, False, True)

    @pl.loop(0, ITERS)
    def _(it):
        sent(traces.at[it, pl.ds(1, n_grp - 1)], it, TRACE)
        sent(rounded.at[it, 0], it, UP)
        sent(rounded.at[it, bx + 1], it, DOWN)
        sent(side.at[it, 0], it, RIGHT)
        sent(side.at[it, 1], it, LEFT)
        sent(zrecv.at[it], it, ZSUM)
        sent(zlow.at[it, pl.ds(1, n_slab - 1)], it, ZALL)
        sent(yrecv.at[it], it, YSUM)
        sent(dot_recv.at[it], it, DOTS)


def shards(axes, *args):
    (
        right_side,
        block_weight,
        across_weight,
        along_weight,
        block_stiffness,
        across_matrix,
        along_matrix,
        boundary_blocks,
        block_rows,
        block_columns,
        live_pairs,
        surface_index,
        interface_slot,
    ) = args
    cases, bx, by, wide = right_side.shape
    pairs = block_rows.shape[-1]
    slots = interface_slot.shape[0]
    surface = surface_index.reshape(-1)
    n_sec, n_clu, n_blk = axes
    n_slab, n_grp, n_all = n_sec * n_clu, n_sec * n_blk, n_sec * n_clu * n_blk
    number = jnp.arange(slots, dtype=jnp.int32)
    slot_inv = jnp.sum(
        jnp.where(interface_slot[:, None] == number[None, :], number[:, None], 0), axis=0
    )
    dofs = jnp.arange(bx * by * wide, dtype=jnp.int32)
    order = jnp.arange(1, wide + 1, dtype=jnp.int32)
    surf_inv = (
        jnp.sum(jnp.where(surface[:, None] == dofs[None, :], order[:, None], 0), axis=0) - 1
    )

    def spread(factor):
        return jnp.broadcast_to(factor[:, :, None, None], factor.shape + (1, wide))

    vmem = pl.BlockSpec(memory_space=pltpu.VMEM)
    smem = pl.BlockSpec(memory_space=pltpu.SMEM)
    field = pltpu.VMEM((bx, by, cases, wide), F32)
    result = pl.pallas_call(
        functools.partial(kernel, axes, (cases, bx, by, wide, pairs)),
        out_shape=jax.ShapeDtypeStruct((cases * bx * by, wide), F32),
        in_specs=[vmem] * 8 + [smem] * 3 + [vmem] * 4,
        out_specs=vmem,
        scratch_shapes=[
            field,
            field,
            field,
            field,
            pltpu.VMEM((ITERS, bx + 2, by, cases, wide), BF16),
            pltpu.VMEM((ITERS, 2, bx, cases, wide), BF16),
            pltpu.VMEM((bx + 1, by, 1, wide), F32),
            pltpu.VMEM((by + 1, bx, 1, wide), F32),
            pltpu.VMEM((ITERS, n_grp, cases, wide), BF16),
            pltpu.VMEM((n_grp, cases, wide), BF16),
            pltpu.VMEM((ITERS, n_slab, cases, wide), F32),
            pltpu.VMEM((ITERS, n_slab - 1, cases, wide), F32),
            pltpu.VMEM((ITERS, n_slab, cases, wide), BF16),
            pltpu.VMEM((n_grp, cases, wide), F32),
            pltpu.VMEM((ITERS, n_grp, cases, wide), F32),
            pltpu.VMEM((ITERS, n_grp - 1, cases, wide), F32),
            pltpu.VMEM((ITERS, 1, wide), F32),
            pltpu.VMEM((ITERS, n_all - 1, 1, wide), F32),
            pltpu.SemaphoreType.DMA((ITERS, 9)),
            pltpu.SemaphoreType.DMA((ITERS, 9)),
            pltpu.SemaphoreType.DMA((2,)),
            pltpu.SemaphoreType.DMA((2,)),
        ],
        compiler_params=pltpu.CompilerParams(
            collective_id=0, has_side_effects=True, vmem_limit_bytes=44 * 1024 * 1024
        ),
        name="conjugate_gradients",
    )(
        right_side.reshape(cases * bx * by, wide),
        spread(block_weight),
        spread(across_weight),
        spread(along_weight.T),
        block_stiffness,
        across_matrix,
        along_matrix,
        boundary_blocks.reshape(pairs, wide, wide),
        block_rows.reshape(1, pairs),
        block_columns.reshape(1, pairs),
        live_pairs.reshape(1, 1),
        surface.reshape(1, wide),
        surf_inv.reshape(bx * by, wide),
        interface_slot.reshape(n_grp, wide),
        slot_inv.reshape(n_grp, wide),
    )
    return result.reshape(right_side.shape)


def solution(mesh):
    axes = tuple(mesh.shape[name] for name in ("sec", "clu", "blk"))
    field = P(None, ("sec", "clu"), "blk", None)
    factor = P(("sec", "clu"), "blk")
    listed = P("sec", "clu", "blk")
    return jax.shard_map(
        functools.partial(shards, axes),
        mesh=mesh,
        in_specs=(
            field,
            factor,
            factor,
            factor,
            P(),
            P(),
            P(),
            P("sec", "clu", "blk", None, None),
            listed,
            listed,
            listed,
            listed,
            P("clu"),
        ),
        out_specs=field,
        check_vma=False,
    )
```

time: 653 us -> 108 us (0.17); the launches traced: 645 us -> 107 us
  blocking collectives: 360 us -> 0 us
  Pallas kernels: 0 us -> 93 us
  local copies, waits for them, and re-layouts: 87.8 us -> 11 us
  waiting for transfers between devices: 55.3 us -> 0 us
  starting transfers between devices: 47.3 us -> 0 us
  other arithmetic: 48 us -> 2.47 us
  matrix products: 31.6 us -> 0 us
  between operations: 14.9 us -> 0.73 us
    psum x8 -> x0, blocking collectives: 283 us -> none  [the longest x3 119 us: squares(): return lax.psum(case_sum(residual, residual), ('sec', 'clu', 'blk'))]
    pallas_call x0 -> x1, Pallas kernels: none -> 93 us  [shards(): pl.pallas_call(functools.partial(kernel, axes, (cases, bx, by, wide, pair...]
    all_gather x3 -> x0, blocking collectives: 76.3 us -> none  [shards(): gathered = lax.all_gather(mine, ('sec', 'blk'), axis=1, tiled=True)]
    reduce_scatter x3 -> x0, waiting for transfers between devices: 52.7 us -> none  [shards(): lax.psum_scatter(jnp.take(partial_rows, inverse, axis=1), ('sec', 'blk'),...]
    ppermute x14 -> x0, starting transfers between devices: 47.2 us -> none  [the longest x6 30.2 us: extended_2(): lax.ppermute(lax.slice_in_dim(block, block.shape[dim] - width, None, axis...]
    gather x15 -> x0, local copies, waits for them, and re-layouts: 42.1 us -> none  [the longest x3 12.9 us: shards(): jnp.take(partial_rows, inverse, axis=1)]
    reshape x13 -> x0, local copies, waits for them, and re-layouts: 32 us -> none  [the longest x4 14.6 us: shards(): image_field = result.reshape(count_cases, -1).at[:, surface_local].add(ow...]
    dot_general x18 -> x0, matrix products: 31.6 us -> none  [the longest x3 10.4 us: shards(): jnp.einsum('cabk,kl->cabl', rounded, block_stiffness, preferred_element_t...]
  transfers between devices with their start and end apart: 17 -> 0, of which waited for: 5 -> 0; matrix products, arithmetic and copies ran while one was open for 16% -> 0% of each run, Pallas kernels for 0% -> 0%
where the time goes in v1:
time: 108 us; the launch traced here: 107 us
  Pallas kernels  93 us (86%)
  local copies, waits for them, and re-layouts  11 us (10%)
  other arithmetic  2.47 us (2%)
    pallas_call x1, Pallas kernels, shards(): pl.pallas_call(functools.partial(kernel, axes, (cases, bx, by, wide, pair...  93 us
    unnamed x19, local copies, waits for them, and re-layouts  8.53 us

profile of v1, /device:TPU:0, one launch (start us, length us, event | category | flops | bytes accessed | tf_op | source)
XLA Modules:
  0.0 107.2 jit_solution(13101107706989099781)
XLA Ops:
  0.7 0.8 copy.15
  1.4 1.2 %select_reduce_fusion = s32[1024]{0:T(1024)S(1)} fusion(s32[1024]{0:T(1024)} %param.25), kind=kLoop, calls=%fused_computation | loop fusion | flops 3144704 | bytes 8192 | tf_op jit(solution)/shard_map/reduce_sum | solution.py:393
  2.6 0.1 broadcast_in_dim.32.along
  2.7 1.3 %select_reduce_fusion.1 = s32[8192]{0:T(1024)S(1)} fusion(s32[128]{0:T(128)S(1)} %iota_add_fusion, s32[128]{0:T(128)} %bitcast.19), kind=kLoop, calls=%fused_computation.2 | loop fusion | flops 3137536 | bytes 33792 | tf_op jit(solution)/shard_map/reduce_sum | solution.py:399
  4.0 0.8 broadcast_in_dim.30.weight
  4.9 0.8 broadcast_in_dim.31.across
  5.7 0.0 copy-start
  5.7 1.4 %copy-done = bf16[1,1,48,128,128]{4,3,2,1,0:T(8,128)(2,1)S(1)} copy-done((bf16[1,1,48,128,128]{4,3,2,1,0:T(8,128)(2,1)S(1)}, bf16[1,1,48,128,128]{4,3,2,1,0:T(8,128)(2,1)}, u32[]{:S(2)}) %copy-start) | copy-done | bytes 1572888
  7.1 0.0 copy-start.1
  7.1 1.2 %copy-done.1 = f32[32,8,8,128]{3,2,1,0:T(8,128)S(1)} copy-done((f32[32,8,8,128]{3,2,1,0:T(8,128)S(1)}, f32[32,8,8,128]{3,2,1,0:T(8,128)}, u32[]{:S(2)}) %copy-start.1) | copy-done | bytes 1048600
  8.3 0.0 copy-start.2
  8.3 0.8 copy-done.2
  9.1 0.0 copy-start.3
  9.1 0.8 copy-done.3
  9.8 0.0 copy-start.4
  9.8 0.8 copy-done.4
  10.6 0.0 copy-start.5
  10.6 0.7 copy-done.5
  11.3 0.0 copy-start.6
  11.3 0.7 copy-done.6
  11.9 0.0 copy-start.7
  11.9 0.7 copy-done.7
  12.6 0.0 copy-start.8
  12.6 0.7 copy-done.8
  13.2 93.0 %conjugate_gradients.1 = f32[2048,128]{1,0:T(8,128)S(1)} custom-call(f32[2048,128]{1,0:T(8,128)S(1)} %bitcast.16, f32[8,8,1,128]{3,2,1,0:T(1,128)S(1)} %broadcast_in_dim.30.weight, f32[8,8,1,128]{3,2,1,0:T(1,128)S(1)} %broadcast_in_dim.31.across, f32[8,8,1,128]{3,2,1,0:T(1,128)S(1)} %broadcast_in_dim.32.along, bf16[128,128]{1,0:T(8,128)(2,1)S(1)} %copy-done.2, ...), custom_call_target="tpu_custom_call" | custom-call | tf_op jit(solution)/shard_map/conjugate_gradients/pallas_call | solution.py:408
  106.3 1.0 copy.18
  (2 shorter events, 0.0 us)
Async XLA Ops:
  5.7 1.4 %copy-start = (bf16[1,1,48,128,128]{4,3,2,1,0:T(8,128)(2,1)S(1)}, bf16[1,1,48,128,128]{4,3,2,1,0:T(8,128)(2,1)}, u32[]{:S(2)}) copy-start(bf16[1,1,48,128,128]{4,3,2,1,0:T(8,128)(2,1)} %param.20) | copy-start | bytes 4718596
  7.1 1.2 %copy-start.1 = (f32[32,8,8,128]{3,2,1,0:T(8,128)S(1)}, f32[32,8,8,128]{3,2,1,0:T(8,128)}, u32[]{:S(2)}) copy-start(f32[32,8,8,128]{3,2,1,0:T(8,128)} %param.13) | copy-start | bytes 3145732
  8.3 0.8 copy-start.2
  9.1 0.8 copy-start.3
  9.8 0.8 copy-start.4
  10.6 0.7 copy-start.5
  11.3 0.7 copy-start.6
  11.9 0.7 copy-start.7
  12.6 0.7 copy-start.8

commit v2 on v1

--- a/solution.py
+++ b/solution.py
@@ -22,22 +22,37 @@
 def kernel(
     axes,
     dims,
+    rhs_hbm,
+    weight_hbm,
+    across_hbm,
+    along_hbm,
+    stiff_hbm,
+    amat_hbm,
+    lmat_hbm,
+    blocks_hbm,
+    surf_hbm,
+    slot_hbm,
+    rows_hbm,
+    cols_hbm,
+    live_hbm,
+    out,
     rhs,
-    weight,
-    across,
-    along,
+    weight_in,
+    across_in,
+    along_in,
     stiff,
     amat,
     lmat,
     blocks,
+    surf,
+    slot,
     rows,
     cols,
     live,
-    surf,
+    weight,
     surf_inv,
-    slot,
+    slot_col,
     slot_inv,
-    out,
     direction,
     residual,
     image,
@@ -60,6 +75,7 @@
     recv_sem,
     edge_send,
     edge_recv,
+    load_sem,
 ):
     n_sec, n_clu, n_blk = axes
     cases, bx, by, wide, pairs = dims
@@ -70,27 +86,67 @@
     me = slab * n_blk + blk
     tile = (cases, wide)
 
+    def turned(position, count, by_):
+        value = position + by_
+        return jnp.where(value >= count, value - count, value)
+
+    secs = [sec if k == 0 else turned(sec, n_sec, k) for k in range(n_sec)]
+    clus = [clu if k == 0 else turned(clu, n_clu, k) for k in range(n_clu)]
+    blks = [blk if k == 0 else turned(blk, n_blk, k) for k in range(n_blk)]
+    slab_peers = [
+        (secs[s] * n_clu + clus[c], (secs[s], clus[c], blk))
+        for s in range(n_sec)
+        for c in range(n_clu)
+        if s or c
+    ]
+    group_peers = [
+        (secs[s] * n_blk + blks[j], (secs[s], clu, blks[j]))
+        for s in range(n_sec)
+        for j in range(n_blk)
+        if s or j
+    ]
+    all_peers = [
+        (secs[s], clus[c], blks[j])
+        for s in range(n_sec)
+        for c in range(n_clu)
+        for j in range(n_blk)
+        if s or c or j
+    ]
+
     def slab_device(index):
         return (index // n_clu, lax.rem(index, n_clu), blk)
-
-    def group_device(index):
-        return (index // n_blk, clu, lax.rem(index, n_blk))
-
-    def any_device(index):
-        return (index // (n_clu * n_blk), lax.rem(index // n_blk, n_clu), lax.rem(index, n_blk))
 
     next_slab = slab_device(lax.rem(slab + 1, n_slab))
     last_slab = slab_device(lax.rem(slab + n_slab - 1, n_slab))
     next_blk = (sec, clu, lax.rem(blk + 1, n_blk))
     last_blk = (sec, clu, lax.rem(blk + n_blk - 1, n_blk))
 
+    loads = [
+        pltpu.make_async_copy(src, dst, load_sem.at[n])
+        for n, (src, dst) in enumerate(
+            (
+                (rhs_hbm, rhs),
+                (surf_hbm, surf),
+                (across_hbm, across_in),
+                (along_hbm, along_in),
+                (weight_hbm, weight_in),
+                (slot_hbm, slot),
+                (rows_hbm, rows),
+                (cols_hbm, cols),
+                (live_hbm, live),
+                (stiff_hbm, stiff),
+                (amat_hbm, amat),
+                (lmat_hbm, lmat),
+                (blocks_hbm, blocks),
+            )
+        )
+    ]
+    for load in loads:
+        load.start()
+
     barrier = pltpu.get_barrier_semaphore()
-
-    @pl.loop(1, n_all)
-    def _(k):
-        pl.semaphore_signal(
-            barrier, inc=1, device_id=any_device(lax.rem(me + k, n_all)), device_id_type=MESH
-        )
+    for device in all_peers:
+        pl.semaphore_signal(barrier, inc=1, device_id=device, device_id_type=MESH)
 
     def send(src, dst, it, phase, device):
         pltpu.make_async_remote_copy(
@@ -108,6 +164,8 @@
     def sent(ref, it, phase):
         pltpu.make_async_copy(ref, ref, send_sem.at[it, phase]).wait()
 
+    for load in loads[:5]:
+        load.wait()
     surf_row = jnp.broadcast_to(surf[...], tile)
     surf_lane = lax.rem(surf_row, wide)
     surf_block = surf_row // wide
@@ -126,18 +184,25 @@
             trace = jnp.where(surf_block == i, lanes(value, surf_lane), trace)
         return square, trace
 
-    square, trace = lax.fori_loop(0, bx, begin, (zero, zero))
-    traces[0, 0] = trace.astype(BF16)
-    across_ext[1:bx] = across[: bx - 1]
-    across_ext[bx] = across[bx - 1] * (slab < n_slab - 1).astype(F32)
-    along_ext[1:by] = along[: by - 1]
-    along_ext[by] = along[by - 1] * (blk < n_blk - 1).astype(F32)
+    square, start = lax.fori_loop(0, bx, begin, (zero, zero), unroll=2)
+    traces[0, group] = start.astype(BF16)
+    inner_slab = (slab < n_slab - 1).astype(F32)
+    inner_blk = (blk < n_blk - 1).astype(F32)
+    for b in range(by):
+        shape = (bx, wide)
+        own_w = jnp.broadcast_to(weight_in[:, b : b + 1], shape)
+        own_a = jnp.broadcast_to(across_in[:, b : b + 1], shape)
+        own_l = jnp.broadcast_to(along_in[:, b : b + 1], shape)
+        for a in range(bx):
+            weight[a, b] = own_w[a : a + 1]
+            across_ext[a + 1, b] = own_a[a : a + 1]
+            along_ext[b + 1, a] = own_l[a : a + 1]
 
     pl.semaphore_wait(barrier, n_all - 1)
 
     edges = (
-        (across.at[bx - 1], across_ext.at[0], 0, next_slab),
-        (along.at[by - 1], along_ext.at[0], 1, next_blk),
+        (across_ext.at[bx], across_ext.at[0], 0, next_slab),
+        (along_ext.at[by], along_ext.at[0], 1, next_blk),
     )
 
     def edge_copy(src, dst, n, device):
@@ -174,23 +239,21 @@
                 sums = [s + jnp.where(goal == q, term, zero) for q, s in enumerate(sums)]
             return tuple(sums)
 
-        return lax.fori_loop(0, pairs // unit, step, (zero,) * count)
+        return lax.fori_loop(0, pairs // unit, step, (zero,) * count, unroll=2)
 
     sublane = lax.broadcasted_iota(jnp.int32, tile, 0)
     lane_id = lax.broadcasted_iota(jnp.int32, tile, 1)
 
-    def iteration(it, square, first, last):
-        @pl.loop(1, n_grp)
-        def _(k):
-            target = lax.rem(group + k, n_grp)
-            send(traces.at[it, 0], traces.at[it, k], it, TRACE, group_device(target))
-
+    def begin_sends(it):
+        for _, device in group_peers:
+            send(traces.at[it, group], traces.at[it, group], it, TRACE, device)
         send(rounded.at[it, bx], rounded.at[it, 0], it, UP, next_slab)
         send(rounded.at[it, 1], rounded.at[it, bx + 1], it, DOWN, last_slab)
         send(rounded.at[it, pl.ds(1, bx), by - 1], side.at[it, 0], it, RIGHT, next_blk)
         send(rounded.at[it, pl.ds(1, bx), 0], side.at[it, 1], it, LEFT, last_blk)
 
-        @pl.loop(0, bx)
+    def iteration(it, square, d_surf, last):
+        @pl.loop(0, bx, unroll=4)
         def _(a):
             own = rounded[it, a + 1].reshape(by * cases, wide)
             part = jnp.dot(own, stiff[...], preferred_element_type=F32)
@@ -198,10 +261,10 @@
 
         received(traces.at[it, pl.ds(1, n_grp - 1)], it, TRACE)
 
-        @pl.loop(0, n_grp)
+        @pl.loop(0, n_grp, unroll=4)
         def _(r):
             def source(k):
-                return traces[it, k].astype(F32), lax.rem(group - k + n_grp, n_grp)
+                return traces[it, k].astype(F32), k
 
             index = jnp.broadcast_to(slot[pl.ds(r, 1), :], tile)
             tiles[r] = permuted(index, n_grp, source).astype(BF16)
@@ -210,17 +273,24 @@
         for q in range(n_slab):
             zpart[it, q] = sums[q]
 
-        @pl.loop(1, n_slab)
-        def _(k):
-            target = lax.rem(slab + k, n_slab)
-            send(zpart.at[it, target], zrecv.at[it, k - 1], it, ZSUM, slab_device(target))
+        for k, (target, device) in enumerate(slab_peers):
+            send(zpart.at[it, target], zrecv.at[it, k], it, ZSUM, device)
+
+        @pl.when(it == 0)
+        def _():
+            for edge in edges:
+                edge_copy(*edge).wait()
+            across_ext[0] = across_ext[0] * (slab > 0).astype(F32)
+            along_ext[0] = along_ext[0] * (blk > 0).astype(F32)
+            across_ext[bx] = across_ext[bx] * inner_slab
+            along_ext[by] = along_ext[by] * inner_blk
 
         received(rounded.at[it, 0], it, UP)
         received(rounded.at[it, bx + 1], it, DOWN)
         received(side.at[it, 0], it, RIGHT)
         received(side.at[it, 1], it, LEFT)
 
-        @pl.loop(0, bx)
+        @pl.loop(0, bx, unroll=4)
         def _(a):
             after = rounded[it, a + 2].reshape(by * cases, wide)
             before = rounded[it, a].reshape(by * cases, wide)
@@ -235,14 +305,11 @@
         column = zpart[it, slab]
         for k in range(n_slab - 1):
             column += zrecv[it, k]
-        zlow[it, 0] = column.astype(BF16)
-
-        @pl.loop(1, n_slab)
-        def _(k):
-            target = lax.rem(slab + k, n_slab)
-            send(zlow.at[it, 0], zlow.at[it, k], it, ZALL, slab_device(target))
-
-        @pl.loop(0, bx)
+        zlow[it, slab] = column.astype(BF16)
+        for _, device in slab_peers:
+            send(zlow.at[it, slab], zlow.at[it, slab], it, ZALL, device)
+
+        @pl.loop(0, bx, unroll=4)
         def _(a):
             right = rounded[it, a + 1, pl.ds(1, by - 1)].reshape((by - 1) * cases, wide)
             left = rounded[it, a + 1, pl.ds(0, by - 1)].reshape((by - 1) * cases, wide)
@@ -257,39 +324,41 @@
 
         received(zlow.at[it, pl.ds(1, n_slab - 1)], it, ZALL)
         sums = pair_sums(
-            lambda e: zlow[it, lax.rem(slab - cols[0, e] + n_slab, n_slab)], rows, n_grp, True
+            lambda e: zlow[it, cols[0, e]], rows, n_grp, True
         )
         for r in range(n_grp):
             ytile[r] = sums[r]
 
-        @pl.loop(0, n_grp)
+        @pl.loop(0, n_grp, unroll=4)
         def _(g):
             index = jnp.broadcast_to(slot_inv[pl.ds(g, 1), :], tile)
             ypart[it, g] = permuted(index, n_grp, lambda k: (ytile[k], k))
 
-        @pl.loop(1, n_grp)
-        def _(k):
-            target = lax.rem(group + k, n_grp)
-            send(ypart.at[it, target], yrecv.at[it, k - 1], it, YSUM, group_device(target))
+        for k, (target, device) in enumerate(group_peers):
+            send(ypart.at[it, target], yrecv.at[it, k], it, YSUM, device)
+
+        def finish(a, carry):
+            d_q, r_q, q_q, r_surf, q_surf = carry
+            for b in range(by):
+                value = image[a, b]
+                rest = residual[a, b]
+                d_q += direction[a, b] * value
+                r_q += rest * value
+                q_q += value * value
+                here = surf_block == a * by + b
+                r_surf = jnp.where(here, lanes(rest, surf_lane), r_surf)
+                q_surf = jnp.where(here, lanes(value, surf_lane), q_surf)
+            return d_q, r_q, q_q, r_surf, q_surf
+
+        d_q, r_q, q_q, r_surf, q_surf = lax.fori_loop(0, bx, finish, (zero,) * 5, unroll=2)
 
         received(yrecv.at[it], it, YSUM)
         own_y = ypart[it, group]
         for k in range(n_grp - 1):
             own_y += yrecv[it, k]
-
-        def finish(a, carry):
-            d_q, r_q, q_q = carry
-            for b in range(by):
-                index = jnp.broadcast_to(surf_inv[pl.ds(a * by + b, 1), :], tile)
-                extra = lanes(own_y, jnp.maximum(index, 0))
-                value = image[a, b] + jnp.where(index >= 0, extra, zero)
-                image[a, b] = value
-                d_q += direction[a, b] * value
-                r_q += residual[a, b] * value
-                q_q += value * value
-            return d_q, r_q, q_q
-
-        d_q, r_q, q_q = lax.fori_loop(0, bx, finish, (zero, zero, zero))
+        d_q += d_surf * own_y
+        r_q += r_surf * own_y
+        q_q += (2.0 * q_surf + own_y) * own_y
 
         packed = zero
         for m, value in enumerate((square, d_q, r_q, q_q)):
@@ -297,10 +366,17 @@
             packed = jnp.where(lane_id == sublane + m * cases, case, packed)
         dot_send[it] = jnp.sum(packed, axis=0, keepdims=True)
 
-        @pl.loop(1, n_all)
-        def _(k):
-            target = any_device(lax.rem(me + k, n_all))
-            send(dot_send.at[it], dot_recv.at[it, k - 1], it, DOTS, target)
+        for k, device in enumerate(all_peers):
+            send(dot_send.at[it], dot_recv.at[it, k], it, DOTS, device)
+
+        if not last:
+
+            @pl.loop(0, bx, unroll=2)
+            def _(a):
+                for b in range(by):
+                    index = jnp.broadcast_to(surf_inv[pl.ds(a * by + b, 1), :], tile)
+                    extra = lanes(own_y, jnp.maximum(index, 0))
+                    image[a, b] += jnp.where(index >= 0, extra, zero)
 
         received(dot_recv.at[it], it, DOTS)
         summed = dot_send[it] + jnp.sum(dot_recv[it], axis=0)
@@ -314,13 +390,13 @@
         alpha = norm / d_q
         if last:
 
-            @pl.loop(0, bx)
+            @pl.loop(0, bx, unroll=2)
             def _(a):
                 for b in range(by):
                     value = total[a, b] + alpha * direction[a, b]
                     out[pl.ds(a * by + b, cases, stride=bx * by), :] = value
 
-            return zero
+            return zero, zero
 
         r_q, q_q = case_value(2), case_value(3)
         norm_next = norm - 2.0 * alpha * r_q + alpha * alpha * q_q
@@ -340,19 +416,43 @@
                 trace = jnp.where(surf_block == a * by + b, lanes(value, surf_lane), trace)
             return square, trace
 
-        square, trace = lax.fori_loop(0, bx, update, (zero, zero))
-        traces[it + 1, 0] = trace.astype(BF16)
-        return square
-
+        square, trace = lax.fori_loop(0, bx, update, (zero, zero), unroll=2)
+        traces[it + 1, group] = trace.astype(BF16)
+        begin_sends(it + 1)
+        return square, trace
+
+    begin_sends(0)
     for edge in edges:
         edge_copy(*edge).start()
-    for edge in edges:
-        edge_copy(*edge).wait()
-    across_ext[0] = across_ext[0] * (slab > 0).astype(F32)
-    along_ext[0] = along_ext[0] * (blk > 0).astype(F32)
-
-    square = lax.fori_loop(0, ITERS - 1, lambda it, s: iteration(it, s, False, False), square)
-    iteration(ITERS - 1, square, False, True)
+    for load in loads[5:]:
+        load.wait()
+
+    square_tile = (wide, wide)
+    down = lax.broadcasted_iota(jnp.int32, square_tile, 0)
+    over = lax.broadcasted_iota(jnp.int32, square_tile, 1)
+    surf_col = jnp.broadcast_to(surf[...], square_tile).T
+
+    @pl.loop(0, bx * by, unroll=4)
+    def _(i):
+        hit = jnp.where(surf_col == over + i * wide, down + 1, 0)
+        surf_inv[pl.ds(i, 1), :] = jnp.sum(hit, axis=0, keepdims=True) - 1
+
+    @pl.loop(0, n_grp)
+    def _(r):
+        slot_col[r] = jnp.broadcast_to(slot[pl.ds(r, 1), :], square_tile).T
+
+    @pl.loop(0, n_grp)
+    def _(g):
+        def step(r, found):
+            return jnp.where(slot_col[r] == over + g * wide, down + r * wide, found)
+
+        found = lax.fori_loop(0, n_grp, step, jnp.zeros(square_tile, jnp.int32), unroll=4)
+        slot_inv[pl.ds(g, 1), :] = jnp.sum(found, axis=0, keepdims=True)
+
+    carry = lax.fori_loop(
+        0, ITERS - 1, lambda it, c: iteration(it, c[0], c[1], False), (square, start)
+    )
+    iteration(ITERS - 1, carry[0], carry[1], True)
 
     @pl.loop(0, ITERS)
     def _(it):
@@ -385,32 +485,35 @@
     ) = args
     cases, bx, by, wide = right_side.shape
     pairs = block_rows.shape[-1]
-    slots = interface_slot.shape[0]
     surface = surface_index.reshape(-1)
     n_sec, n_clu, n_blk = axes
     n_slab, n_grp, n_all = n_sec * n_clu, n_sec * n_blk, n_sec * n_clu * n_blk
-    number = jnp.arange(slots, dtype=jnp.int32)
-    slot_inv = jnp.sum(
-        jnp.where(interface_slot[:, None] == number[None, :], number[:, None], 0), axis=0
-    )
-    dofs = jnp.arange(bx * by * wide, dtype=jnp.int32)
-    order = jnp.arange(1, wide + 1, dtype=jnp.int32)
-    surf_inv = (
-        jnp.sum(jnp.where(surface[:, None] == dofs[None, :], order[:, None], 0), axis=0) - 1
-    )
-
-    def spread(factor):
-        return jnp.broadcast_to(factor[:, :, None, None], factor.shape + (1, wide))
-
+    hbm = pl.BlockSpec(memory_space=pltpu.HBM)
     vmem = pl.BlockSpec(memory_space=pltpu.VMEM)
-    smem = pl.BlockSpec(memory_space=pltpu.SMEM)
     field = pltpu.VMEM((bx, by, cases, wide), F32)
     result = pl.pallas_call(
         functools.partial(kernel, axes, (cases, bx, by, wide, pairs)),
         out_shape=jax.ShapeDtypeStruct((cases * bx * by, wide), F32),
-        in_specs=[vmem] * 8 + [smem] * 3 + [vmem] * 4,
+        in_specs=[hbm] * 13,
         out_specs=vmem,
         scratch_shapes=[
+            pltpu.VMEM((cases * bx * by, wide), F32),
+            pltpu.VMEM((bx, by), F32),
+            pltpu.VMEM((bx, by), F32),
+            pltpu.VMEM((bx, by), F32),
+            pltpu.VMEM((wide, wide), BF16),
+            pltpu.VMEM((wide, wide), BF16),
+            pltpu.VMEM((wide, wide), BF16),
+            pltpu.VMEM((pairs, wide, wide), BF16),
+            pltpu.VMEM((1, wide), jnp.int32),
+            pltpu.VMEM((n_grp, wide), jnp.int32),
+            pltpu.SMEM((1, pairs), jnp.int32),
+            pltpu.SMEM((1, pairs), jnp.int32),
+            pltpu.SMEM((1, 1), jnp.int32),
+            pltpu.VMEM((bx, by, 1, wide), F32),
+            pltpu.VMEM((bx * by, wide), jnp.int32),
+            pltpu.VMEM((n_grp, wide, wide), jnp.int32),
+            pltpu.VMEM((n_grp, wide), jnp.int32),
             field,
             field,
             field,
@@ -433,6 +536,7 @@
             pltpu.SemaphoreType.DMA((ITERS, 9)),
             pltpu.SemaphoreType.DMA((2,)),
             pltpu.SemaphoreType.DMA((2,)),
+            pltpu.SemaphoreType.DMA((13,)),
         ],
         compiler_params=pltpu.CompilerParams(
             collective_id=0, has_side_effects=True, vmem_limit_bytes=44 * 1024 * 1024
@@ -440,20 +544,18 @@
         name="conjugate_gradients",
     )(
         right_side.reshape(cases * bx * by, wide),
-        spread(block_weight),
-        spread(across_weight),
-        spread(along_weight.T),
+        block_weight,
+        across_weight,
+        along_weight,
         block_stiffness,
         across_matrix,
         along_matrix,
         boundary_blocks.reshape(pairs, wide, wide),
+        surface.reshape(1, wide),
+        interface_slot.reshape(n_grp, wide),
         block_rows.reshape(1, pairs),
         block_columns.reshape(1, pairs),
         live_pairs.reshape(1, 1),
-        surface.reshape(1, wide),
-        surf_inv.reshape(bx * by, wide),
-        interface_slot.reshape(n_grp, wide),
-        slot_inv.reshape(n_grp, wide),
     )
     return result.reshape(right_side.shape)
 

time: 108 us -> 91 us (0.84)
  Pallas kernels: 93 us -> 79.2 us
  other arithmetic: 2.47 us -> 0 us
    pallas_call x1, Pallas kernels: 93 us -> 79.2 us  [shards(): pl.pallas_call(functools.partial(kernel, axes, (cases, bx, by, wide, pair...]
    reduce_sum x2 -> x0, other arithmetic: 2.46 us -> none  [the longest x1 1.28 us: shards(): jnp.sum(jnp.where(surface[:, None] == dofs[None, :], order[:, None], 0),...]
    unnamed x19 -> x25, local copies, waits for them, and re-layouts: 8.53 us -> 10.6 us
    broadcast_in_dim x3 -> x0, local copies, waits for them, and re-layouts: 1.74 us -> none  [spread(): return jnp.broadcast_to(factor[:, :, None, None], factor.shape + (1, wide))]
where the time goes in v2:
time: 91 us; the launch traced here: 90.4 us
  Pallas kernels  79.2 us (87%)
  local copies, waits for them, and re-layouts  10.6 us (12%)
    pallas_call x1, Pallas kernels, shards(): pl.pallas_call(functools.partial(kernel, axes, (cases, bx, by, wide, pair...  79.2 us
    unnamed x25, local copies, waits for them, and re-layouts  10.6 us

profile of v2, /device:TPU:0, one launch (start us, length us, event | category | flops | bytes accessed | tf_op | source)
XLA Modules:
  0.0 90.4 jit_solution(10712808137880421080)
XLA Ops:
  0.7 0.0 copy-start
  0.7 1.4 %copy-done = bf16[1,1,48,128,128]{4,3,2,1,0:T(8,128)(2,1)S(1)} copy-done((bf16[1,1,48,128,128]{4,3,2,1,0:T(8,128)(2,1)S(1)}, bf16[1,1,48,128,128]{4,3,2,1,0:T(8,128)(2,1)}, u32[]{:S(2)}) %copy-start) | copy-done | bytes 1572888
  2.1 0.0 copy-start.1
  2.1 1.2 %copy-done.1 = f32[32,8,8,128]{3,2,1,0:T(8,128)S(1)} copy-done((f32[32,8,8,128]{3,2,1,0:T(8,128)S(1)}, f32[32,8,8,128]{3,2,1,0:T(8,128)}, u32[]{:S(2)}) %copy-start.1) | copy-done | bytes 1048600
  3.3 0.0 copy-start.2
  3.3 0.8 copy-done.2
  4.0 0.0 copy-start.3
  4.0 0.8 copy-done.3
  4.8 0.0 copy-start.4
  4.8 0.8 copy-done.4
  5.6 0.0 copy-start.5
  5.6 0.7 copy-done.5
  6.2 0.0 copy-start.6
  6.3 0.7 copy-done.6
  6.9 0.0 copy-start.7
  6.9 0.7 copy-done.7
  7.6 0.0 copy-start.8
  7.6 0.7 copy-done.8
  8.3 0.0 copy-start.9
  8.3 0.7 copy-done.9
  9.0 0.0 copy-start.10
  9.0 0.7 copy-done.10
  9.6 0.0 copy-start.11
  9.6 0.7 copy-done.11
  10.3 79.2 %conjugate_gradients.1 = f32[2048,128]{1,0:T(8,128)S(1)} custom-call(f32[2048,128]{1,0:T(8,128)S(1)} %bitcast.11, f32[8,8]{1,0:T(8,128)S(1)} %copy-done.5, f32[8,8]{1,0:T(8,128)S(1)} %copy-done.6, f32[8,8]{1,0:T(8,128)S(1)} %copy-done.7, bf16[128,128]{1,0:T(8,128)(2,1)S(1)} %copy-done.2, bf16[128,128]{1,0:T(8,128)(2,1)S(1)} %copy-done.3, ...), custom_call_target="tpu_custom_call" | custom-call | tf_op jit(solution)/shard_map/conjugate_gradients/pallas_call | solution.py:494
  89.5 1.0 %copy.16 = f32[32,8,8,128]{3,2,1,0:T(8,128)} copy(f32[32,8,8,128]{3,2,1,0:T(8,128)S(1)} %bitcast.9) | data formatting | bytes 2097152
Async XLA Ops:
  0.7 1.4 %copy-start = (bf16[1,1,48,128,128]{4,3,2,1,0:T(8,128)(2,1)S(1)}, bf16[1,1,48,128,128]{4,3,2,1,0:T(8,128)(2,1)}, u32[]{:S(2)}) copy-start(bf16[1,1,48,128,128]{4,3,2,1,0:T(8,128)(2,1)} %param.20) | copy-start | bytes 4718596
  2.1 1.2 %copy-start.1 = (f32[32,8,8,128]{3,2,1,0:T(8,128)S(1)}, f32[32,8,8,128]{3,2,1,0:T(8,128)}, u32[]{:S(2)}) copy-start(f32[32,8,8,128]{3,2,1,0:T(8,128)} %param.13) | copy-start | bytes 3145732
  3.3 0.8 copy-start.2
  4.0 0.8 copy-start.3
  4.8 0.8 copy-start.4
  5.6 0.7 copy-start.5
  6.2 0.7 copy-start.6
  6.9 0.7 copy-start.7
  7.6 0.7 copy-start.8
  8.3 0.7 copy-start.9
  9.0 0.7 copy-start.10
  9.6 0.7 copy-start.11

commit v3 on v2

--- a/solution.py
+++ b/solution.py
@@ -49,6 +49,9 @@
     rows,
     cols,
     live,
+    amat_t,
+    lmat_t,
+    blocks_t,
     weight,
     surf_inv,
     slot_col,
@@ -121,6 +124,9 @@
     next_blk = (sec, clu, lax.rem(blk + 1, n_blk))
     last_blk = (sec, clu, lax.rem(blk + n_blk - 1, n_blk))
 
+    has_last, has_next = slab > 0, slab < n_slab - 1
+    has_left, has_right = blk > 0, blk < n_blk - 1
+
     loads = [
         pltpu.make_async_copy(src, dst, load_sem.at[n])
         for n, (src, dst) in enumerate(
@@ -186,8 +192,24 @@
 
     square, start = lax.fori_loop(0, bx, begin, (zero, zero), unroll=2)
     traces[0, group] = start.astype(BF16)
-    inner_slab = (slab < n_slab - 1).astype(F32)
-    inner_blk = (blk < n_blk - 1).astype(F32)
+    for there, ref in ((has_last, across_ext), (has_left, along_ext)):
+
+        @pl.when(jnp.logical_not(there))
+        def _(ref=ref):
+            ref[0] = jnp.zeros(ref.shape[1:], F32)
+
+    for it in range(ITERS):
+        for there, halo, place in (
+            (has_last, rounded, 0),
+            (has_next, rounded, bx + 1),
+            (has_left, side, 0),
+            (has_right, side, 1),
+        ):
+
+            @pl.when(jnp.logical_not(there))
+            def _(halo=halo, place=place, it=it):
+                halo[it, place] = jnp.zeros(halo.shape[2:], BF16)
+
     for b in range(by):
         shape = (bx, wide)
         own_w = jnp.broadcast_to(weight_in[:, b : b + 1], shape)
@@ -233,9 +255,10 @@
             for u in range(unit):
                 e = i * unit + u
                 left = pick(e)
-                dims_ = (((1,), (1 if flip else 0,)), ((), ()))
-                term = lax.dot_general(left, blocks[e], dims_, preferred_element_type=F32)
-                goal = jnp.where(e < live[0, 0], into[0, e], -1)
+                block = blocks_t[e] if flip else blocks[e]
+                term = jnp.dot(left, block, preferred_element_type=F32)
+                goal = jnp.where(e < live[0, 0, 0], into[0, e], -1)
+                goal = jnp.full(tile, goal, jnp.int32)
                 sums = [s + jnp.where(goal == q, term, zero) for q, s in enumerate(sums)]
             return tuple(sums)
 
@@ -247,10 +270,22 @@
     def begin_sends(it):
         for _, device in group_peers:
             send(traces.at[it, group], traces.at[it, group], it, TRACE, device)
-        send(rounded.at[it, bx], rounded.at[it, 0], it, UP, next_slab)
-        send(rounded.at[it, 1], rounded.at[it, bx + 1], it, DOWN, last_slab)
-        send(rounded.at[it, pl.ds(1, bx), by - 1], side.at[it, 0], it, RIGHT, next_blk)
-        send(rounded.at[it, pl.ds(1, bx), 0], side.at[it, 1], it, LEFT, last_blk)
+
+        @pl.when(has_next)
+        def _():
+            send(rounded.at[it, bx], rounded.at[it, 0], it, UP, next_slab)
+
+        @pl.when(has_last)
+        def _():
+            send(rounded.at[it, 1], rounded.at[it, bx + 1], it, DOWN, last_slab)
+
+        @pl.when(has_right)
+        def _():
+            send(rounded.at[it, pl.ds(1, bx), by - 1], side.at[it, 0], it, RIGHT, next_blk)
+
+        @pl.when(has_left)
+        def _():
+            send(rounded.at[it, pl.ds(1, bx), 0], side.at[it, 1], it, LEFT, last_blk)
 
     def iteration(it, square, d_surf, last):
         @pl.loop(0, bx, unroll=4)
@@ -278,17 +313,26 @@
 
         @pl.when(it == 0)
         def _():
-            for edge in edges:
-                edge_copy(*edge).wait()
-            across_ext[0] = across_ext[0] * (slab > 0).astype(F32)
-            along_ext[0] = along_ext[0] * (blk > 0).astype(F32)
-            across_ext[bx] = across_ext[bx] * inner_slab
-            along_ext[by] = along_ext[by] * inner_blk
-
-        received(rounded.at[it, 0], it, UP)
-        received(rounded.at[it, bx + 1], it, DOWN)
-        received(side.at[it, 0], it, RIGHT)
-        received(side.at[it, 1], it, LEFT)
+            for edge, onward, back in zip(edges, (has_next, has_right), (has_last, has_left)):
+
+                @pl.when(onward)
+                def _(edge=edge):
+                    edge_copy(*edge).wait_send()
+
+                @pl.when(back)
+                def _(edge=edge):
+                    edge_copy(*edge).wait_recv()
+
+        for there, ref, phase in (
+            (has_last, rounded.at[it, 0], UP),
+            (has_next, rounded.at[it, bx + 1], DOWN),
+            (has_left, side.at[it, 0], RIGHT),
+            (has_right, side.at[it, 1], LEFT),
+        ):
+
+            @pl.when(there)
+            def _(ref=ref, phase=phase):
+                received(ref, it, phase)
 
         @pl.loop(0, bx, unroll=4)
         def _(a):
@@ -296,9 +340,7 @@
             before = rounded[it, a].reshape(by * cases, wide)
             part = jnp.dot(after, amat[...], preferred_element_type=F32)
             value = image[a] - across_ext[a + 1] * part.reshape(by, cases, wide)
-            part = lax.dot_general(
-                before, amat[...], (((1,), (1,)), ((), ())), preferred_element_type=F32
-            )
+            part = jnp.dot(before, amat_t[...], preferred_element_type=F32)
             image[a] = value - across_ext[a] * part.reshape(by, cases, wide)
 
         received(zrecv.at[it], it, ZSUM)
@@ -317,9 +359,7 @@
             before = jnp.concatenate([side[it, 0, a], left], axis=0)
             part = jnp.dot(after, lmat[...], preferred_element_type=F32)
             value = image[a] - along_ext[pl.ds(1, by), a] * part.reshape(by, cases, wide)
-            part = lax.dot_general(
-                before, lmat[...], (((1,), (1,)), ((), ())), preferred_element_type=F32
-            )
+            part = jnp.dot(before, lmat_t[...], preferred_element_type=F32)
             image[a] = value - along_ext[pl.ds(0, by), a] * part.reshape(by, cases, wide)
 
         received(zlow.at[it, pl.ds(1, n_slab - 1)], it, ZALL)
@@ -422,10 +462,21 @@
         return square, trace
 
     begin_sends(0)
-    for edge in edges:
-        edge_copy(*edge).start()
+    for edge, onward in zip(edges, (has_next, has_right)):
+
+        @pl.when(onward)
+        def _(edge=edge):
+            edge_copy(*edge).start()
+
     for load in loads[5:]:
         load.wait()
+
+    amat_t[...] = amat[...].T
+    lmat_t[...] = lmat[...].T
+
+    @pl.loop(0, pairs, unroll=4)
+    def _(e):
+        blocks_t[e] = blocks[e].T
 
     square_tile = (wide, wide)
     down = lax.broadcasted_iota(jnp.int32, square_tile, 0)
@@ -457,10 +508,16 @@
     @pl.loop(0, ITERS)
     def _(it):
         sent(traces.at[it, pl.ds(1, n_grp - 1)], it, TRACE)
-        sent(rounded.at[it, 0], it, UP)
-        sent(rounded.at[it, bx + 1], it, DOWN)
-        sent(side.at[it, 0], it, RIGHT)
-        sent(side.at[it, 1], it, LEFT)
+        for there, ref, phase in (
+            (has_next, rounded.at[it, 0], UP),
+            (has_last, rounded.at[it, bx + 1], DOWN),
+            (has_right, side.at[it, 0], RIGHT),
+            (has_left, side.at[it, 1], LEFT),
+        ):
+
+            @pl.when(there)
+            def _(ref=ref, phase=phase):
+                sent(ref, it, phase)
         sent(zrecv.at[it], it, ZSUM)
         sent(zlow.at[it, pl.ds(1, n_slab - 1)], it, ZALL)
         sent(yrecv.at[it], it, YSUM)
@@ -509,7 +566,10 @@
             pltpu.VMEM((n_grp, wide), jnp.int32),
             pltpu.SMEM((1, pairs), jnp.int32),
             pltpu.SMEM((1, pairs), jnp.int32),
-            pltpu.SMEM((1, 1), jnp.int32),
+            pltpu.SMEM((1, 1, 1), jnp.int32),
+            pltpu.VMEM((wide, wide), BF16),
+            pltpu.VMEM((wide, wide), BF16),
+            pltpu.VMEM((pairs, wide, wide), BF16),
             pltpu.VMEM((bx, by, 1, wide), F32),
             pltpu.VMEM((bx * by, wide), jnp.int32),
             pltpu.VMEM((n_grp, wide, wide), jnp.int32),
@@ -539,7 +599,7 @@
             pltpu.SemaphoreType.DMA((13,)),
         ],
         compiler_params=pltpu.CompilerParams(
-            collective_id=0, has_side_effects=True, vmem_limit_bytes=44 * 1024 * 1024
+            collective_id=0, has_side_effects=True, vmem_limit_bytes=62 * 1024 * 1024
         ),
         name="conjugate_gradients",
     )(
@@ -555,7 +615,7 @@
         interface_slot.reshape(n_grp, wide),
         block_rows.reshape(1, pairs),
         block_columns.reshape(1, pairs),
-        live_pairs.reshape(1, 1),
+        live_pairs,
     )
     return result.reshape(right_side.shape)
 

time: 91 us -> 80.5 us (0.88)
  local copies, waits for them, and re-layouts: 10.6 us -> 2.31 us
  Pallas kernels: 79.2 us -> 77.4 us
    unnamed x25 -> x1, local copies, waits for them, and re-layouts: 10.6 us -> 2.31 us
    pallas_call x1, Pallas kernels: 79.2 us -> 77.4 us  [shards(): pl.pallas_call(functools.partial(kernel, axes, (cases, bx, by, wide, pair...]
where the time goes in v3:
time: 80.5 us; the launch traced here: 80.3 us
  Pallas kernels  77.4 us (96%)
  local copies, waits for them, and re-layouts  2.31 us (3%)
    pallas_call x1, Pallas kernels, shards(): pl.pallas_call(functools.partial(kernel, axes, (cases, bx, by, wide, pair...  77.4 us
    unnamed x1, local copies, waits for them, and re-layouts  2.31 us

profile of v3, /device:TPU:0, one launch (start us, length us, event | category | flops | bytes accessed | tf_op | source)
XLA Modules:
  0.0 80.3 jit_solution(10038372062663115718)
XLA Ops:
  0.7 77.4 %conjugate_gradients.1 = f32[2048,128]{1,0:T(8,128)} custom-call(f32[2048,128]{1,0:T(8,128)} %bitcast.9, f32[8,8]{1,0:T(8,128)} %weight_hbm.1, f32[8,8]{1,0:T(8,128)} %across_hbm.1, f32[8,8]{1,0:T(8,128)} %along_hbm.1, bf16[128,128]{1,0:T(8,128)(2,1)} %stiff_hbm.1, bf16[128,128]{1,0:T(8,128)(2,1)} %amat_hbm.1, bf16[128,128]{1,0:T(8,128)(2,1)} %lmat_hbm.1, ...), custom_call_target="tpu_custom_call" | custom-call | tf_op jit(solution)/shard_map/conjugate_gradients/pallas_call | solution.py:551
  78.0 2.3 %copy.16 = f32[32,8,8,128]{3,2,1,0:T(8,128)} copy(f32[32,8,8,128]{3,2,1,0:T(8,128)} %bitcast.7) | data formatting | bytes 2097152

commit v4 on v3

--- a/solution.py
+++ b/solution.py
@@ -238,7 +238,7 @@
         )
 
     def permuted(index_row, count, source):
-        lane = lax.rem(index_row, wide)
+        lane = index_row & (wide - 1)
         part = index_row // wide
 
         def step(k, value):
@@ -262,7 +262,7 @@
                 sums = [s + jnp.where(goal == q, term, zero) for q, s in enumerate(sums)]
             return tuple(sums)
 
-        return lax.fori_loop(0, pairs // unit, step, (zero,) * count, unroll=2)
+        return lax.fori_loop(0, pairs // unit, step, (zero,) * count, unroll=3)
 
     sublane = lax.broadcasted_iota(jnp.int32, tile, 0)
     lane_id = lax.broadcasted_iota(jnp.int32, tile, 1)
@@ -383,6 +383,8 @@
                 value = image[a, b]
                 rest = residual[a, b]
                 d_q += direction[a, b] * value
+                if last:
+                    continue
                 r_q += rest * value
                 q_q += value * value
                 here = surf_block == a * by + b

time: 80.5 us -> 79.7 us (0.990)
  Pallas kernels: 77.4 us -> 76.5 us
    pallas_call x1, Pallas kernels: 77.4 us -> 76.5 us  [shards(): pl.pallas_call(functools.partial(kernel, axes, (cases, bx, by, wide, pair...]
where the time goes in v4:
time: 79.7 us; the launch traced here: 79.5 us
  Pallas kernels  76.5 us (96%)
  local copies, waits for them, and re-layouts  2.31 us (3%)
    pallas_call x1, Pallas kernels, shards(): pl.pallas_call(functools.partial(kernel, axes, (cases, bx, by, wide, pair...  76.5 us
    unnamed x1, local copies, waits for them, and re-layouts  2.31 us

profile of v4, /device:TPU:0, one launch (start us, length us, event | category | flops | bytes accessed | tf_op | source)
XLA Modules:
  0.0 79.5 jit_solution(16962328967289658729)
XLA Ops:
  0.7 76.5 %conjugate_gradients.1 = f32[2048,128]{1,0:T(8,128)} custom-call(f32[2048,128]{1,0:T(8,128)} %bitcast.9, f32[8,8]{1,0:T(8,128)} %weight_hbm.1, f32[8,8]{1,0:T(8,128)} %across_hbm.1, f32[8,8]{1,0:T(8,128)} %along_hbm.1, bf16[128,128]{1,0:T(8,128)(2,1)} %stiff_hbm.1, bf16[128,128]{1,0:T(8,128)(2,1)} %amat_hbm.1, bf16[128,128]{1,0:T(8,128)(2,1)} %lmat_hbm.1, ...), custom_call_target="tpu_custom_call" | custom-call | tf_op jit(solution)/shard_map/conjugate_gradients/pallas_call | solution.py:553
  77.2 2.3 %copy.16 = f32[32,8,8,128]{3,2,1,0:T(8,128)} copy(f32[32,8,8,128]{3,2,1,0:T(8,128)} %bitcast.7) | data formatting | bytes 2097152
